TPU v7x, 32 devices: a whole 2x2x4 slice. The times are simulated.
32 devices in a mesh: row: 4 (over x, core), col: 8 (over z, y).
Axes of the slice: x: 2, y: 2, z: 4, core: 2. Of those that a mesh axis runs over, the one named last changes fastest.
Arguments:
- coefficients: float32 [8, 8192, 8192], P(None, 'row', 'col'), may hold values from -40 to 40, as said below
- lambdas: float32 [256], replicated, may hold values from -0.95 to 0.95
- right_vecs: float32 [8192, 256], P(('col', 'row')), may hold values from -6 to 6
- left_vecs: float32 [8192, 256], P(('row', 'col')), may hold values from -6 to 6
Outputs:
- right_resid: float32 [8192, 256], P(('row', 'col'))
- left_resid: float32 [8192, 256], P(('col', 'row'))
- root_mean: float32 [2, 256], replicated
Inputs may be any that keep to these rules, and one draw needn't show every extreme that they name: `coefficients`: the entries of every coefficient matrix.
All inputs are finite; a program needn't handle non-finite values.
Results may differ from a plain program's by a relative error of at most 0.0001.
Values sent between devices are 32-bit elements; how exact they have to be, the bound alone decides.
No kernel may reach another device: no remote copies, remote signals or barrier semaphores. Data moves between devices by JAX's collectives and lax.ppermute only.
A program may use at most 128 MiB of HBM per device.

v0:
```python
import jax
import jax.numpy as jnp
from jax import lax
from jax.sharding import PartitionSpec as P

N = 8192


epsilon = 1e-06


def chebyshev(lambdas, count):
    terms = [jnp.ones_like(lambdas), lambdas]
    while len(terms) < count:
        terms.append(2.0 * lambdas * terms[-1] - terms[-2])
    return jnp.stack(terms[:count])


def right_term(matrices, weighted):
    return jnp.einsum(
        "kij,kjm->im",
        matrices,
        weighted,
        precision=lax.Precision.HIGHEST,
        preferred_element_type=jnp.float32,
    )


def left_term(matrices, weighted):
    return jnp.einsum(
        "kij,kim->jm",
        matrices,
        weighted,
        precision=lax.Precision.HIGHEST,
        preferred_element_type=jnp.float32,
    )


def body(coefficients, lambdas, right_vecs, left_vecs):
    weights = chebyshev(lambdas, coefficients.shape[0])
    right_cols = lax.all_gather(right_vecs, "row", axis=0, tiled=True)
    left_rows = lax.all_gather(left_vecs, "col", axis=0, tiled=True)
    right_weighted = right_cols[None, :, :] * weights[:, None, :]
    left_weighted = left_rows[None, :, :] * weights[:, None, :]
    matrices = coefficients
    right_resid = lax.psum_scatter(
        right_term(matrices, right_weighted), "col", scatter_dimension=0, tiled=True
    )
    matrices = coefficients
    left_resid = lax.psum_scatter(
        left_term(matrices, left_weighted), "row", scatter_dimension=0, tiled=True
    )
    right_squares, left_squares = lax.psum(
        (jnp.sum(right_resid * right_resid, axis=0), jnp.sum(left_resid * left_resid, axis=0)),
        ("row", "col"),
    )
    root_mean = jnp.sqrt(jnp.stack([right_squares, left_squares]) / N + epsilon)
    return (right_resid, left_resid, root_mean)


def solution(mesh):
    return jax.shard_map(
        body,
        mesh=mesh,
        in_specs=(P(None, "row", "col"), P(), P(("col", "row"), None), P(("row", "col"), None)),
        out_specs=(P(("row", "col"), None), P(("col", "row"), None), P()),
        check_vma=False,
    )
```

profile of v0, /device:TPU:0, one launch (start us, length us, event | category | flops | bytes accessed | tf_op | source)
XLA Modules:
  0.0 240.2 jit_solution(2977413053173540334)
XLA Ops:
  7.2 0.0 all-gather.3.cloned.1.call-start
  7.2 0.7 all-gather.3.cloned.1.call-update
  7.9 0.0 all-gather.5.cloned.1.call-start
  7.9 0.7 all-gather.5.cloned.1.call-update
  8.6 0.0 reduce-scatter.3.cloned.1.call-start
  8.7 0.7 multiply_subtract_fusion
  9.4 0.7 multiply_subtract_fusion.1
  10.1 0.7 stack.40
  10.8 18.2 %all-gather.3.cloned.1.call-done = f32[1024,256]{1,0:T(8,128)} async-done(((f32[256,256]{1,0:T(8,128)}), f32[1024,256]{1,0:T(8,128)}) %all-gather.3.cloned.1.call-update) | async-done | bytes 1048592 | tf_op jit(solution)/shard_map/all_gather | solution.py:41
  29.0 1.6 copy.7
  30.6 0.6 fusion.24
  31.2 62.3 %fusion.8 = f32[2048,256]{0,1:T(8,128)} fusion(f32[8,2048,1024]{2,1,0:T(8,128)} %param.4, f32[8,1024,256]{1,2,0:T(8,128)S(1)} %fusion.24), kind=kOutput, calls=%fused_computation.8 | convolution fusion | flops 51539607552 | bytes 77594624 | tf_op jit(solution)/shard_map/kij,kjm->im/dot_general | solution.py:20
  93.5 0.0 reduce-scatter.3.cloned.1.call-update
  93.5 0.2 reduce-scatter.5.cloned.1.call-start
  93.7 0.0 all-gather.5.cloned.1.call-done
  93.8 1.9 copy.8
  95.7 6.9 %fusion.26 = f32[8,2048,256]{1,2,0:T(8,128)} fusion(f32[8,256]{1,0:T(8,128)S(1)} %stack.40, f32[2048,256]{0,1:T(8,128)S(1)} %copy.8), kind=kLoop, calls=%fused_computation.1.clone.clone.clone.1 | loop fusion | flops 4194304 | bytes 18882560 | tf_op jit(solution)/shard_map/kij,kim->jm/dot_general | solution.py:30
  102.6 63.2 %fusion.11 = f32[1024,256]{0,1:T(8,128)} fusion(f32[8,2048,1024]{2,1,0:T(8,128)} %param.4, f32[8,2048,256]{1,2,0:T(8,128)} %fusion.26), kind=kOutput, calls=%fused_computation.9 | convolution fusion | flops 51539607552 | bytes 84934656 | tf_op jit(solution)/shard_map/kij,kim->jm/dot_general | solution.py:30
  165.7 0.0 reduce-scatter.5.cloned.1.call-update
  165.8 0.0 reduce-scatter.3.cloned.1.call-done
  165.8 1.8 copy.9
  167.6 1.1 multiply_reduce_fusion.1
  168.6 22.2 %reduce-scatter.5.cloned.1.call-done = f32[256,256]{0,1:T(8,128)} async-done(((f32[1024,256]{0,1:T(8,128)}), f32[256,256]{0,1:T(8,128)}) %reduce-scatter.5.cloned.1.call-update) | async-done | bytes 262160 | tf_op jit(solution)/shard_map/reduce_scatter | solution.py:50
  190.8 1.1 multiply_reduce_fusion
  191.9 39.4 %all-reduce = (f32[1,256]{1,0:T(1,128)S(1)}, f32[1,256]{1,0:T(1,128)S(1)}) all-reduce(f32[1,256]{1,0:T(1,128)S(1)} %bitcast.28, f32[1,256]{1,0:T(1,128)S(1)} %bitcast.27), channel_id=1, replica_groups=mesh['row'=4,'col'=8] {'row','col'}, use_global_device_ids=true, to_apply=%region_5.0 | all-reduce | flops 512 | bytes 4096 | tf_op jit(solution)/shard_map/psum | solution.py:53
  231.3 0.6 fusion.15
  231.9 1.8 copy.10
  (1 shorter events, 0.0 us)
Async XLA Ops:
  7.2 21.8 %all-gather.3.cloned.1.call-start = ((), (), s32[]{:S(2)}) async-start(), calls=%async_computation.2 | async-start | bytes 1310720 | tf_op jit(solution)/shard_map/all_gather | solution.py:41
  7.9 85.8 %all-gather.5.cloned.1.call-start = ((), (), s32[]{:S(2)}) async-start(), calls=%async_computation.4 | async-start | bytes 2359296 | tf_op jit(solution)/shard_map/all_gather | solution.py:42
  8.6 157.1 %reduce-scatter.3.cloned.1.call-start = ((), (), s32[]{:S(2)}) async-start(), calls=%async_computation.3 | async-start | bytes 2359296 | tf_op jit(solution)/shard_map/reduce_scatter | solution.py:46
  93.5 97.3 %reduce-scatter.5.cloned.1.call-start = ((), (), s32[]{:S(2)}) async-start(), calls=%async_computation.5 | async-start | bytes 1310720 | tf_op jit(solution)/shard_map/reduce_scatter | solution.py:50
Sparse Core Ops, SparseCore 0:
  9.6 19.4 all-gather.2
  31.1 49.2 all-gather.4
  93.6 68.1 reduce-scatter.2
  165.9 24.9 reduce-scatter.4
where the time goes:
time: 241 us; the launch traced here: 240 us
  matrix products  125 us (52%)
  waiting for transfers between devices  41.9 us (17%)
  blocking collectives  39.4 us (16%)
  between operations  13.8 us (6%)
  other arithmetic  11.6 us (5%)
  local copies, waits for them, and re-layouts  7.76 us (3%)
    dot_general x1, matrix products, left_term(): jnp.einsum('kij,kim->jm', matrices, weighted, precision=lax.Precision.HIG...  63.2 us
    dot_general x1, matrix products, right_term(): jnp.einsum('kij,kjm->im', matrices, weighted, precision=lax.Precision.HIG...  62.3 us
    psum x1, blocking collectives, body(): lax.psum((jnp.sum(right_resid * right_resid, axis=0), jnp.sum(left_resid...  39.4 us
    reduce_scatter x1, waiting for transfers between devices, body(): lax.psum_scatter(left_term(matrices, left_weighted), 'row', scatter_dimen...  22.2 us
    all_gather x1, waiting for transfers between devices, body(): right_cols = lax.all_gather(right_vecs, 'row', axis=0, tiled=True)  18.2 us
    dot_general x1, other arithmetic, left_term(): jnp.einsum('kij,kim->jm', matrices, weighted, precision=lax.Precision.HIG...  6.89 us
  transfers between devices with their start and end apart: 4, of which 2 were waited for; matrix products, arithmetic and copies ran while one was open for 59% of the time, Pallas kernels for 0%

commit v1 on v0

v1 whole, which is shorter than its diff:
```python
import functools
import jax
import jax.numpy as jnp
from jax import lax
from jax.experimental import pallas as pl
from jax.experimental.pallas import tpu as pltpu
from jax.sharding import PartitionSpec as P

LANES = 128
SLOTS = 3
VMEM_LIMIT = 48 * 2**20

epsilon = 1e-06


def chebyshev(lambdas, count):
    terms = [jnp.ones_like(lambdas), lambdas]
    while len(terms) < count:
        terms.append(2.0 * lambdas * terms[-1] - terms[-2])
    return jnp.stack(terms[:count])


def ring_order(count):
    return list(range(0, count, 2)) + list(range(1, count, 2))[::-1]


def halves(values):
    high = values.astype(jnp.bfloat16)
    return high, (values - high.astype(jnp.float32)).astype(jnp.bfloat16)


def product(left, right, dims):
    def dot(a, b):
        return lax.dot_general(a, b, (dims, ((), ())), preferred_element_type=jnp.float32)

    (left_high, left_low), (right_high, right_low) = left, right
    return dot(left_high, right_high) + dot(left_high, right_low) + dot(left_low, right_high)


def block_copies(matrices_ref, place, buffer, sem):
    width = buffer.shape[2]
    columns = pl.ds(pl.multiple_of(place * width, width), width)

    def copy(term):
        slot = lax.rem(term, SLOTS)
        return pltpu.make_async_copy(matrices_ref.at[term, :, columns], buffer.at[slot], sem.at[slot])

    return copy


def each_matrix(count, copy, step):
    def visit(term, carry):
        copy(term).wait()
        ahead = term + SLOTS - 1

        @pl.when((term > 0) & (ahead < count))
        def _():
            copy(ahead).start()

        step(term)
        return carry

    lax.fori_loop(0, count, visit, 0)


def right_kernel(order, has_total, place_ref, matrices_ref, vecs_ref, weights_ref, *rest):
    total_ref = rest[0] if has_total else None
    out_ref, high, low, buffer, sem, total_sem = rest[-6:]
    count, rows, _ = matrices_ref.shape
    chunk = rows // len(order)
    copy = block_copies(matrices_ref, place_ref[0], buffer, sem)
    for term in range(min(SLOTS, count)):
        copy(jnp.int32(term)).start()
    if has_total:
        fetch = pltpu.make_async_copy(total_ref, out_ref, total_sem)
        fetch.start()
    else:
        out_ref[...] = jnp.zeros_like(out_ref)

    def weigh(term, carry):
        high[term], low[term] = halves(vecs_ref[...] * weights_ref[pl.ds(term, 1), :])
        return carry

    lax.fori_loop(0, count, weigh, 0)
    if has_total:
        fetch.wait()

    def step(term):
        terms = product(halves(buffer[lax.rem(term, SLOTS)]), (high[term], low[term]), ((1,), (0,)))
        for at, member in enumerate(order):
            out_ref[at * chunk : (at + 1) * chunk, :] += terms[member * chunk : (member + 1) * chunk, :]

    each_matrix(count, copy, step)


def left_kernel(order, place_ref, matrices_ref, vecs_ref, weights_ref, out_ref, buffer, sem):
    count, rows, _ = matrices_ref.shape
    chunk = rows // len(order)
    copy = block_copies(matrices_ref, place_ref[0], buffer, sem)
    for term in range(min(SLOTS, count)):
        copy(jnp.int32(term)).start()
    out_ref[...] = jnp.zeros_like(out_ref)
    at = [order.index(member) for member in range(len(order))]

    def step(term):
        vecs = jnp.concatenate([vecs_ref[i * chunk : (i + 1) * chunk, :] for i in at], axis=0)
        weighted = halves(vecs * weights_ref[pl.ds(term, 1), :])
        out_ref[...] += product(halves(buffer[lax.rem(term, SLOTS)]), weighted, ((0,), (0,)))

    each_matrix(count, copy, step)


VMEM = pl.BlockSpec(memory_space=pltpu.VMEM)
SMEM = pl.BlockSpec(memory_space=pltpu.SMEM)
ANY = pl.BlockSpec(memory_space=pl.ANY)


def cost(count, rows, width, trip):
    return pl.CostEstimate(
        flops=6 * count * rows * width * trip, bytes_accessed=4 * count * rows * width, transcendentals=0
    )


def right_terms(order, matrices, vecs, weights, place, total=None):
    count, rows, _ = matrices.shape
    width, trip = vecs.shape
    return pl.pallas_call(
        functools.partial(right_kernel, order, total is not None),
        out_shape=jax.ShapeDtypeStruct((rows, trip), jnp.float32),
        in_specs=[SMEM, ANY, VMEM, VMEM] + ([ANY] if total is not None else []),
        out_specs=VMEM,
        scratch_shapes=[
            pltpu.VMEM((count, width, trip), jnp.bfloat16),
            pltpu.VMEM((count, width, trip), jnp.bfloat16),
            pltpu.VMEM((SLOTS, rows, width), jnp.float32),
            pltpu.SemaphoreType.DMA((SLOTS,)),
            pltpu.SemaphoreType.DMA,
        ],
        compiler_params=pltpu.CompilerParams(vmem_limit_bytes=VMEM_LIMIT),
        cost_estimate=cost(count, rows, width, trip),
        name="right_terms",
    )(jnp.reshape(place, (1,)), matrices, vecs, weights, *([total] if total is not None else []))


def left_terms(order, matrices, vecs, weights, place, width):
    count, rows, _ = matrices.shape
    trip = vecs.shape[1]
    return pl.pallas_call(
        functools.partial(left_kernel, order),
        out_shape=jax.ShapeDtypeStruct((width, trip), jnp.float32),
        in_specs=[SMEM, ANY, VMEM, VMEM],
        out_specs=VMEM,
        scratch_shapes=[
            pltpu.VMEM((SLOTS, rows, width), jnp.float32),
            pltpu.SemaphoreType.DMA((SLOTS,)),
        ],
        compiler_params=pltpu.CompilerParams(vmem_limit_bytes=VMEM_LIMIT),
        cost_estimate=cost(count, rows, width, trip),
        name="left_terms",
    )(jnp.reshape(place, (1,)), matrices, vecs, weights)


def exchange(values, axis, size, bit):
    return lax.ppermute(values, axis, [(i, i ^ bit) for i in range(size)])


def squares(values):
    return jnp.sum(values * values, axis=0)


def body(n_row, n_col, coefficients, lambdas, right_vecs, left_vecs):
    order = ring_order(n_col)
    weights = chebyshev(lambdas, coefficients.shape[0])
    share = right_vecs.shape[0]
    pair = 2 * share
    left_rows = lax.all_gather(left_vecs, "col", axis=0, tiled=True, axis_index_groups=[order])

    row = lax.axis_index("row").astype(jnp.int32)
    core = lax.rem(row, 2)
    if n_row == 4 and pair % LANES == 0:
        here = row // 2
        there = 1 - here

        def in_order(mine, other):
            return jnp.where(core == 0, jnp.concatenate([mine, other]), jnp.concatenate([other, mine]))

        far = exchange(right_vecs, "row", n_row, 2)
        near_vecs = in_order(right_vecs, exchange(right_vecs, "row", n_row, 1))
        right = right_terms(order, coefficients, near_vecs, weights, here)
        far_vecs = in_order(far, exchange(far, "row", n_row, 1))
        right = right_terms(order, coefficients, far_vecs, weights, there, right)
    else:
        right_cols = lax.all_gather(right_vecs, "row", axis=0, tiled=True)
        right = right_terms(order, coefficients, right_cols, weights, jnp.int32(0))
    right_resid = lax.psum_scatter(right, "col", scatter_dimension=0, tiled=True, axis_index_groups=[order])

    if n_row == 4 and pair % LANES == 0:
        sent = left_terms(order, coefficients, left_rows, weights, there, pair)
        came = exchange(sent, "row", n_row, 2)
        kept = left_terms(order, coefficients, left_rows, weights, here, pair)

        def part(values, which):
            return lax.dynamic_slice_in_dim(values, which * share, share, 0)

        other = part(kept, 1 - core) + part(came, 1 - core)
        left_resid = part(kept, core) + part(came, core) + exchange(other, "row", n_row, 1)
    else:
        left = left_terms(order, coefficients, left_rows, weights, jnp.int32(0), n_row * share)
        left_resid = lax.psum_scatter(left, "row", scatter_dimension=0, tiled=True)

    sums = jnp.stack([squares(right_resid), squares(left_resid)])
    devices = n_row * n_col
    copies = jnp.broadcast_to(sums[None], (devices,) + sums.shape)
    parts = lax.all_to_all(copies, ("row", "col"), split_axis=0, concat_axis=0, tiled=True)
    rows = coefficients.shape[1] * n_row
    root_mean = jnp.sqrt(jnp.sum(parts, axis=0) / rows + epsilon)
    return (right_resid, left_resid, root_mean)


def solution(mesh):
    return jax.shard_map(
        functools.partial(body, mesh.shape["row"], mesh.shape["col"]),
        mesh=mesh,
        in_specs=(P(None, "row", "col"), P(), P(("col", "row"), None), P(("row", "col"), None)),
        out_specs=(P(("row", "col"), None), P(("col", "row"), None), P()),
        check_vma=False,
    )
```

time: 241 us -> 116 us (0.48)
  matrix products: 125 us -> 0 us
  Pallas kernels: 0 us -> 70.2 us
  waiting for transfers between devices: 41.9 us -> 7.01 us
  blocking collectives: 39.4 us -> 12 us
  other arithmetic: 11.6 us -> 4.95 us
  local copies, waits for them, and re-layouts: 7.76 us -> 2.31 us
  starting transfers between devices: 0.34 us -> 5.32 us
    dot_general x2 -> x0, matrix products: 125 us -> none  [the longest x1 63.2 us: left_term(): jnp.einsum('kij,kim->jm', matrices, weighted, precision=lax.Precision.HIG...]
    pallas_call x0 -> x4, Pallas kernels: none -> 70.2 us  [the longest x2 35.2 us: left_terms(): pl.pallas_call(functools.partial(left_kernel, order), out_shape=jax.Shape...]
    psum x1 -> x0, blocking collectives: 39.4 us -> none  [body(): lax.psum((jnp.sum(right_resid * right_resid, axis=0), jnp.sum(left_resid...]
    reduce_scatter x2 -> x1, waiting for transfers between devices: 22.2 us -> 0.01 us  [body(): lax.psum_scatter(right, 'col', scatter_dimension=0, tiled=True, axis_inde...]
    all_gather x2 -> x1, waiting for transfers between devices: 18.2 us -> 0.02 us  [body(): lax.all_gather(left_vecs, 'col', axis=0, tiled=True, axis_index_groups=[o...]
    all_to_all x0 -> x1, blocking collectives: none -> 12 us  [body(): lax.all_to_all(copies, ('row', 'col'), split_axis=0, concat_axis=0, tiled...]
    dot_general x2 -> x0, other arithmetic: 7.49 us -> none  [the longest x1 6.89 us: left_term(): jnp.einsum('kij,kim->jm', matrices, weighted, precision=lax.Precision.HIG...]
    ppermute x0 -> x5, waiting for transfers between devices: none -> 6.29 us  [exchange(): return lax.ppermute(values, axis, [(i, i ^ bit) for i in range(size)])]
  transfers between devices with their start and end apart: 4 -> 7, of which waited for: 2 -> 2; matrix products, arithmetic and copies ran while one was open for 59% -> 3% of each run, Pallas kernels for 0% -> 61%
where the time goes in v1:
time: 116 us
  Pallas kernels  70.2 us (61%)
  between operations  14.1 us (12%)
  blocking collectives  12 us (10%)
  waiting for transfers between devices  7.01 us (6%)
  starting transfers between devices  5.32 us (5%)
  other arithmetic  4.95 us (4%)
  local copies, waits for them, and re-layouts  2.31 us (2%)
    pallas_call x2, Pallas kernels, left_terms(): pl.pallas_call(functools.partial(left_kernel, order), out_shape=jax.Shape...  35.2 us
    pallas_call x2, Pallas kernels, right_terms(): pl.pallas_call(functools.partial(right_kernel, order, total is not None),...  35 us
    all_to_all x1, blocking collectives, body(): lax.all_to_all(copies, ('row', 'col'), split_axis=0, concat_axis=0, tiled...  12 us
    ppermute x5, waiting for transfers between devices, exchange(): return lax.ppermute(values, axis, [(i, i ^ bit) for i in range(size)])  6.29 us
    ppermute x5, starting transfers between devices, exchange(): return lax.ppermute(values, axis, [(i, i ^ bit) for i in range(size)])  5.25 us
  transfers between devices with their start and end apart: 7, of which 2 were waited for; matrix products, arithmetic and copies ran while one was open for 3% of the time, Pallas kernels for 61%

profile of v1, /device:TPU:0, one launch (start us, length us, event | category | flops | bytes accessed | tf_op | source)
XLA Modules:
  0.0 116.0 jit_solution(12544449344911565269)
XLA Ops:
  7.2 0.0 all-gather.2.cloned.1.call-start
  7.2 0.7 all-gather.2.cloned.1.call-update
  7.9 0.0 reduce-scatter.2.cloned.1.call-start
  7.9 0.5 collective-permute-start.2
  8.5 2.6 %collective-permute-start = (f32[256,256]{1,0:T(8,128)}, f32[256,256]{1,0:T(8,128)S(1)}, u32[]{:S(2)}, u32[]{:S(2)}) collective-permute-start(f32[256,256]{1,0:T(8,128)} %param.6), channel_id=1, source_target_pairs={{0,16},{8,24},{16,0},{24,8},{1,17},{9,25},{17,1},{25,9},{2,18},{10... | collective-permute-start | bytes 786440 | tf_op jit(solution)/shard_map/ppermute | solution.py:164
  11.0 0.7 multiply_subtract_fusion
  11.7 0.7 multiply_subtract_fusion.1
  12.4 0.7 stack.40.weights_ref
  13.1 5.0 %collective-permute-done = f32[256,256]{1,0:T(8,128)S(1)} collective-permute-done((f32[256,256]{1,0:T(8,128)}, f32[256,256]{1,0:T(8,128)S(1)}, u32[]{:S(2)}, u32[]{:S(2)}) %collective-permute-start) | collective-permute-done | bytes 262176 | tf_op jit(solution)/shard_map/ppermute | solution.py:164
  18.1 0.0 collective-permute-start.1
  18.1 0.0 collective-permute-done.2
  18.1 1.1 maximum_select_fusion.1.vecs_ref
  19.2 16.9 %right_terms.2.rest_0_ = f32[2048,256]{1,0:T(8,128)S(1)} custom-call(s32[1]{0:T(128)} %bitcast.8.place_ref, f32[8,2048,1024]{2,1,0:T(8,128)} %matrices_ref.7, f32[512,256]{1,0:T(8,128)S(1)} %maximum_select_fusion.1.vecs_ref, f32[8,256]{1,0:T(8,128)S(1)} %stack.40.weights_ref), custom_call_target="tpu_custom_call" | custom-call | flops 12884901888 | bytes 33554432 | tf_op jit(solution)/shard_map/right_terms/pallas_call | solution.py:127
  36.1 0.0 collective-permute-done.1
  36.2 18.1 %right_terms.3 = f32[2048,256]{1,0:T(8,128)} custom-call(s32[1]{0:T(128)} %bitcast.place_ref, f32[8,2048,1024]{2,1,0:T(8,128)} %matrices_ref.7, f32[512,256]{1,0:T(8,128)S(1)} %maximum_select_fusion.vecs_ref, f32[8,256]{1,0:T(8,128)S(1)} %stack.40.weights_ref, f32[2048,256]{1,0:T(8,128)S(1)} %right_terms.2.rest_0_), custom_call_target="tpu_custom_call" | custom-call | flops 12884901888 | bytes 33554432 | tf_op jit(solution)/shard_map/right_terms/pallas_call | solution.py:127
  54.3 0.0 reduce-scatter.2.cloned.1.call-update
  54.3 0.0 all-gather.2.cloned.1.call-done.vecs_ref
  54.3 0.0 copy-start
  54.3 1.6 %copy-done = f32[2048,256]{1,0:T(8,128)S(1)} copy-done((f32[2048,256]{1,0:T(8,128)S(1)}, f32[2048,256]{1,0:T(8,128)}, u32[]{:S(2)}) %copy-start) | copy-done | bytes 2097176
  55.9 17.6 %left_terms.3 = f32[512,256]{1,0:T(8,128)S(1)} custom-call(s32[1]{0:T(128)} %bitcast.place_ref, f32[8,2048,1024]{2,1,0:T(8,128)} %matrices_ref.7, f32[2048,256]{1,0:T(8,128)S(1)} %copy-done, f32[8,256]{1,0:T(8,128)S(1)} %stack.40.weights_ref), custom_call_target="tpu_custom_call" | custom-call | flops 12884901888 | bytes 33554432 | tf_op jit(solution)/shard_map/left_terms/pallas_call | solution.py:148
  73.5 1.8 %collective-permute-start.3 = (f32[512,256]{1,0:T(8,128)S(1)}, f32[512,256]{1,0:T(8,128)S(1)}, u32[]{:S(2)}, u32[]{:S(2)}) collective-permute-start(f32[512,256]{1,0:T(8,128)S(1)} %left_terms.3), channel_id=1, source_target_pairs={{0,16},{8,24},{16,0},{24,8},{1,17},{9,25},{17,1},{25,9},{2,18},{10... | collective-permute-start | bytes 1572872 | tf_op jit(solution)/shard_map/ppermute | solution.py:164
  75.4 17.6 %left_terms.2 = f32[512,256]{1,0:T(8,128)S(1)} custom-call(s32[1]{0:T(128)} %bitcast.8.place_ref, f32[8,2048,1024]{2,1,0:T(8,128)} %matrices_ref.7, f32[2048,256]{1,0:T(8,128)S(1)} %copy-done, f32[8,256]{1,0:T(8,128)S(1)} %stack.40.weights_ref), custom_call_target="tpu_custom_call" | custom-call | flops 12884901888 | bytes 33554432 | tf_op jit(solution)/shard_map/left_terms/pallas_call | solution.py:148
  93.0 0.0 collective-permute-done.3
  93.1 0.3 collective-permute-start.4
  93.4 1.3 %collective-permute-done.4 = f32[256,256]{1,0:T(8,128)S(1)} collective-permute-done((f32[256,256]{1,0:T(8,128)S(1)}, f32[256,256]{1,0:T(8,128)S(1)}, u32[]{:S(2)}, u32[]{:S(2)}) %collective-permute-start.4) | collective-permute-done | bytes 262176 | tf_op jit(solution)/shard_map/ppermute | solution.py:164
  94.7 0.8 multiply_reduce_fusion
  95.4 0.0 reduce-scatter.2.cloned.1.call-done
  95.4 1.0 multiply_reduce_fusion.1
  96.5 12.0 %all_to_all.5 = f32[32,2,256]{2,1,0:T(2,128)S(1)} all-to-all(f32[32,2,256]{2,1,0:T(2,128)S(1)} %broadcast_in_dim.2), channel_id=1, replica_groups=mesh['row'=4,'col'=8] {'row','col'}, dimensions={0} | all-to-all | bytes 131072 | tf_op jit(solution)/shard_map/all_to_all | solution.py:214
  108.5 0.6 add_sqrt_fusion
  (6 shorter events, 0.2 us)
Async XLA Ops:
  7.2 47.2 %all-gather.2.cloned.1.call-start = ((), (), s32[]{:S(2)}) async-start(), calls=%async_computation.3 | async-start | bytes 2359296 | tf_op jit(solution)/shard_map/all_gather | solution.py:176
  7.9 87.5 %reduce-scatter.2.cloned.1.call-start = ((), (), s32[]{:S(2)}) async-start(), calls=%async_computation.2 | async-start | bytes 2359296 | tf_op jit(solution)/shard_map/reduce_scatter | solution.py:195
  7.9 10.2 %collective-permute-start.2 = (f32[256,256]{1,0:T(8,128)}, f32[256,256]{1,0:T(8,128)S(1)}, u32[]{:S(2)}, u32[]{:S(2)}) collective-permute-start(f32[256,256]{1,0:T(8,128)} %param.6), channel_id=1, source_target_pairs={{0,8},{8,0},{16,24},{24,16},{1,9},{9,1},{17,25},{25,17},{2,10},{10... | collective-permute-start | bytes 786440 | tf_op jit(solution)/shard_map/ppermute | solution.py:164
  8.5 9.7 %collective-permute-start = (f32[256,256]{1,0:T(8,128)}, f32[256,256]{1,0:T(8,128)S(1)}, u32[]{:S(2)}, u32[]{:S(2)}) collective-permute-start(f32[256,256]{1,0:T(8,128)} %param.6), channel_id=1, source_target_pairs={{0,16},{8,24},{16,0},{24,8},{1,17},{9,25},{17,1},{25,9},{2,18},{10... | collective-permute-start | bytes 786440 | tf_op jit(solution)/shard_map/ppermute | solution.py:164
  18.1 18.0 %collective-permute-start.1 = (f32[256,256]{1,0:T(8,128)S(1)}, f32[256,256]{1,0:T(8,128)S(1)}, u32[]{:S(2)}, u32[]{:S(2)}) collective-permute-start(f32[256,256]{1,0:T(8,128)S(1)} %collective-permute-done), channel_id=1, source_target_pairs={{0,8},{8,0},{16,24},{24,16},{1,9},{9,1},{17,25},{25,17},{2,10},{10... | collective-permute-start | bytes 786440 | tf_op jit(solution)/shard_map/ppermute | solution.py:164
  54.3 1.6 %copy-start = (f32[2048,256]{1,0:T(8,128)S(1)}, f32[2048,256]{1,0:T(8,128)}, u32[]{:S(2)}) copy-start(f32[2048,256]{1,0:T(8,128)} %all-gather.2.cloned.1.call-done.vecs_ref) | copy-start | bytes 6291460
  73.5 19.5 %collective-permute-start.3 = (f32[512,256]{1,0:T(8,128)S(1)}, f32[512,256]{1,0:T(8,128)S(1)}, u32[]{:S(2)}, u32[]{:S(2)}) collective-permute-start(f32[512,256]{1,0:T(8,128)S(1)} %left_terms.3), channel_id=1, source_target_pairs={{0,16},{8,24},{16,0},{24,8},{1,17},{9,25},{17,1},{25,9},{2,18},{10... | collective-permute-start | bytes 1572872 | tf_op jit(solution)/shard_map/ppermute | solution.py:164
  93.1 1.6 %collective-permute-start.4 = (f32[256,256]{1,0:T(8,128)S(1)}, f32[256,256]{1,0:T(8,128)S(1)}, u32[]{:S(2)}, u32[]{:S(2)}) collective-permute-start(f32[256,256]{1,0:T(8,128)S(1)} %dynamic-slice_add_fusion), channel_id=1, source_target_pairs={{0,8},{8,0},{16,24},{24,16},{1,9},{9,1},{17,25},{25,17},{2,10},{10... | collective-permute-start | bytes 786440 | tf_op jit(solution)/shard_map/ppermute | solution.py:164
Sparse Core Ops, SparseCore 0:
  9.5 36.0 all-gather.1
  54.4 34.6 reduce-scatter.1

commit v2 on v1

--- a/solution.py
+++ b/solution.py
@@ -64,26 +64,19 @@
 
 
 def right_kernel(order, has_total, place_ref, matrices_ref, vecs_ref, weights_ref, *rest):
-    total_ref = rest[0] if has_total else None
-    out_ref, high, low, buffer, sem, total_sem = rest[-6:]
+    out_ref, high, low, buffer, sem = rest[-5:]
     count, rows, _ = matrices_ref.shape
     chunk = rows // len(order)
     copy = block_copies(matrices_ref, place_ref[0], buffer, sem)
     for term in range(min(SLOTS, count)):
         copy(jnp.int32(term)).start()
-    if has_total:
-        fetch = pltpu.make_async_copy(total_ref, out_ref, total_sem)
-        fetch.start()
-    else:
-        out_ref[...] = jnp.zeros_like(out_ref)
+    out_ref[...] = rest[0][...] if has_total else jnp.zeros_like(out_ref)
 
     def weigh(term, carry):
         high[term], low[term] = halves(vecs_ref[...] * weights_ref[pl.ds(term, 1), :])
         return carry
 
     lax.fori_loop(0, count, weigh, 0)
-    if has_total:
-        fetch.wait()
 
     def step(term):
         terms = product(halves(buffer[lax.rem(term, SLOTS)]), (high[term], low[term]), ((1,), (0,)))
@@ -127,14 +120,13 @@
     return pl.pallas_call(
         functools.partial(right_kernel, order, total is not None),
         out_shape=jax.ShapeDtypeStruct((rows, trip), jnp.float32),
-        in_specs=[SMEM, ANY, VMEM, VMEM] + ([ANY] if total is not None else []),
+        in_specs=[SMEM, ANY, VMEM, VMEM] + ([VMEM] if total is not None else []),
         out_specs=VMEM,
         scratch_shapes=[
             pltpu.VMEM((count, width, trip), jnp.bfloat16),
             pltpu.VMEM((count, width, trip), jnp.bfloat16),
             pltpu.VMEM((SLOTS, rows, width), jnp.float32),
             pltpu.SemaphoreType.DMA((SLOTS,)),
-            pltpu.SemaphoreType.DMA,
         ],
         compiler_params=pltpu.CompilerParams(vmem_limit_bytes=VMEM_LIMIT),
         cost_estimate=cost(count, rows, width, trip),
@@ -180,14 +172,10 @@
     if n_row == 4 and pair % LANES == 0:
         here = row // 2
         there = 1 - here
-
-        def in_order(mine, other):
-            return jnp.where(core == 0, jnp.concatenate([mine, other]), jnp.concatenate([other, mine]))
-
-        far = exchange(right_vecs, "row", n_row, 2)
-        near_vecs = in_order(right_vecs, exchange(right_vecs, "row", n_row, 1))
+        other = exchange(right_vecs, "row", n_row, 1)
+        near_vecs = jnp.where(core == 0, jnp.concatenate([right_vecs, other]), jnp.concatenate([other, right_vecs]))
+        far_vecs = exchange(near_vecs, "row", n_row, 2)
         right = right_terms(order, coefficients, near_vecs, weights, here)
-        far_vecs = in_order(far, exchange(far, "row", n_row, 1))
         right = right_terms(order, coefficients, far_vecs, weights, there, right)
     else:
         right_cols = lax.all_gather(right_vecs, "row", axis=0, tiled=True)

time: 116 us -> 111 us (0.957)
  waiting for transfers between devices: 7.01 us -> 2.01 us
  starting transfers between devices: 5.32 us -> 3.57 us
  blocking collectives: 12 us -> 13.5 us
    ppermute x5 -> x4, waiting for transfers between devices: 6.29 us -> 1.29 us  [exchange(): return lax.ppermute(values, axis, [(i, i ^ bit) for i in range(size)])]
    ppermute x5 -> x4, starting transfers between devices: 5.25 us -> 3.49 us  [exchange(): return lax.ppermute(values, axis, [(i, i ^ bit) for i in range(size)])]
    all_to_all x1, blocking collectives: 12 us -> 13.5 us  [body(): lax.all_to_all(copies, ('row', 'col'), split_axis=0, concat_axis=0, tiled...]
  transfers between devices with their start and end apart: 7 -> 6, of which waited for: 2 -> 1; matrix products, arithmetic and copies ran while one was open for 3% -> 4% of each run, Pallas kernels for 61% -> 63%
where the time goes in v2:
time: 111 us
  Pallas kernels  70.2 us (63%)
  between operations  14.1 us (13%)
  blocking collectives  13.5 us (12%)
  other arithmetic  4.91 us (4%)
  starting transfers between devices  3.57 us (3%)
  local copies, waits for them, and re-layouts  2.31 us (2%)
  waiting for transfers between devices  2.01 us (2%)
    pallas_call x2, Pallas kernels, left_terms(): pl.pallas_call(functools.partial(left_kernel, order), out_shape=jax.Shape...  35.2 us
    pallas_call x2, Pallas kernels, right_terms(): pl.pallas_call(functools.partial(right_kernel, order, total is not None),...  35 us
    all_to_all x1, blocking collectives, body(): lax.all_to_all(copies, ('row', 'col'), split_axis=0, concat_axis=0, tiled...  13.5 us
    ppermute x4, starting transfers between devices, exchange(): return lax.ppermute(values, axis, [(i, i ^ bit) for i in range(size)])  3.49 us
  transfers between devices with their start and end apart: 6, of which 1 were waited for; matrix products, arithmetic and copies ran while one was open for 4% of the time, Pallas kernels for 63%

profile of v2, /device:TPU:0, one launch (start us, length us, event | category | flops | bytes accessed | tf_op | source)
XLA Modules:
  0.0 110.6 jit_solution(6514339754355436)
XLA Ops:
  7.2 0.0 all-gather.2.cloned.1.call-start
  7.2 0.7 all-gather.2.cloned.1.call-update
  7.9 0.0 reduce-scatter.2.cloned.1.call-start
  7.9 0.5 collective-permute-start
  8.5 0.7 multiply_subtract_fusion
  9.2 0.7 multiply_subtract_fusion.1
  9.8 0.7 stack.40.weights_ref
  10.6 0.0 collective-permute-done
  10.6 1.1 maximum_select_fusion.vecs_ref
  11.6 2.6 %collective-permute-start.1 = (f32[512,256]{1,0:T(8,128)S(1)}, f32[512,256]{1,0:T(8,128)S(1)}, u32[]{:S(2)}, u32[]{:S(2)}) collective-permute-start(f32[512,256]{1,0:T(8,128)S(1)} %maximum_select_fusion.vecs_ref), channel_id=1, source_target_pairs={{0,16},{8,24},{16,0},{24,8},{1,17},{9,25},{17,1},{25,9},{2,18},{10... | collective-permute-start | bytes 1572872 | tf_op jit(solution)/shard_map/ppermute | solution.py:156
  14.2 16.9 %right_terms.2.rest_0_ = f32[2048,256]{1,0:T(8,128)S(1)} custom-call(s32[1]{0:T(128)} %bitcast.8.place_ref, f32[8,2048,1024]{2,1,0:T(8,128)} %matrices_ref.7, f32[512,256]{1,0:T(8,128)S(1)} %maximum_select_fusion.vecs_ref, f32[8,256]{1,0:T(8,128)S(1)} %stack.40.weights_ref), custom_call_target="tpu_custom_call" | custom-call | flops 12884901888 | bytes 33554432 | tf_op jit(solution)/shard_map/right_terms/pallas_call | solution.py:120
  31.1 0.0 collective-permute-done.1.vecs_ref
  31.1 18.1 %right_terms.3 = f32[2048,256]{1,0:T(8,128)} custom-call(s32[1]{0:T(128)} %bitcast.place_ref, f32[8,2048,1024]{2,1,0:T(8,128)} %matrices_ref.7, f32[512,256]{1,0:T(8,128)S(1)} %collective-permute-done.1.vecs_ref, f32[8,256]{1,0:T(8,128)S(1)} %stack.40.weights_ref, f32[2048,256]{1,0:T(8,128)S(1)} %right_terms.2.rest_0_), custom_call_target="tpu_custom_call" | custom-call | flops 12884901888 | bytes 33554432 | tf_op jit(solution)/shard_map/right_terms/pallas_call | solution.py:120
  49.2 0.0 reduce-scatter.2.cloned.1.call-update
  49.2 0.0 all-gather.2.cloned.1.call-done.vecs_ref
  49.3 0.0 copy-start
  49.3 1.6 %copy-done = f32[2048,256]{1,0:T(8,128)S(1)} copy-done((f32[2048,256]{1,0:T(8,128)S(1)}, f32[2048,256]{1,0:T(8,128)}, u32[]{:S(2)}) %copy-start) | copy-done | bytes 2097176
  50.8 17.6 %left_terms.3 = f32[512,256]{1,0:T(8,128)S(1)} custom-call(s32[1]{0:T(128)} %bitcast.place_ref, f32[8,2048,1024]{2,1,0:T(8,128)} %matrices_ref.7, f32[2048,256]{1,0:T(8,128)S(1)} %copy-done, f32[8,256]{1,0:T(8,128)S(1)} %stack.40.weights_ref), custom_call_target="tpu_custom_call" | custom-call | flops 12884901888 | bytes 33554432 | tf_op jit(solution)/shard_map/left_terms/pallas_call | solution.py:140
  68.5 0.1 collective-permute-start.2
  68.6 17.6 %left_terms.2 = f32[512,256]{1,0:T(8,128)S(1)} custom-call(s32[1]{0:T(128)} %bitcast.8.place_ref, f32[8,2048,1024]{2,1,0:T(8,128)} %matrices_ref.7, f32[2048,256]{1,0:T(8,128)S(1)} %copy-done, f32[8,256]{1,0:T(8,128)S(1)} %stack.40.weights_ref), custom_call_target="tpu_custom_call" | custom-call | flops 12884901888 | bytes 33554432 | tf_op jit(solution)/shard_map/left_terms/pallas_call | solution.py:140
  86.2 0.0 collective-permute-done.2
  86.3 0.3 collective-permute-start.3
  86.6 1.3 %collective-permute-done.3 = f32[256,256]{1,0:T(8,128)S(1)} collective-permute-done((f32[256,256]{1,0:T(8,128)S(1)}, f32[256,256]{1,0:T(8,128)S(1)}, u32[]{:S(2)}, u32[]{:S(2)}) %collective-permute-start.3) | collective-permute-done | bytes 262176 | tf_op jit(solution)/shard_map/ppermute | solution.py:156
  87.9 0.8 multiply_reduce_fusion
  88.6 0.0 reduce-scatter.2.cloned.1.call-done
  88.6 1.0 multiply_reduce_fusion.1
  89.6 13.5 %all_to_all.5 = f32[32,2,256]{2,1,0:T(2,128)S(1)} all-to-all(f32[32,2,256]{2,1,0:T(2,128)S(1)} %broadcast_in_dim.2), channel_id=1, replica_groups=mesh['row'=4,'col'=8] {'row','col'}, dimensions={0} | all-to-all | bytes 131072 | tf_op jit(solution)/shard_map/all_to_all | solution.py:202
  103.2 0.6 add_sqrt_fusion
  (5 shorter events, 0.1 us)
Async XLA Ops:
  7.2 42.1 %all-gather.2.cloned.1.call-start = ((), (), s32[]{:S(2)}) async-start(), calls=%async_computation.3 | async-start | bytes 2359296 | tf_op jit(solution)/shard_map/all_gather | solution.py:168
  7.9 80.7 %reduce-scatter.2.cloned.1.call-start = ((), (), s32[]{:S(2)}) async-start(), calls=%async_computation.2 | async-start | bytes 2359296 | tf_op jit(solution)/shard_map/reduce_scatter | solution.py:183
  7.9 2.6 %collective-permute-start = (f32[256,256]{1,0:T(8,128)}, f32[256,256]{1,0:T(8,128)S(1)}, u32[]{:S(2)}, u32[]{:S(2)}) collective-permute-start(f32[256,256]{1,0:T(8,128)} %param.6), channel_id=1, source_target_pairs={{0,8},{8,0},{16,24},{24,16},{1,9},{9,1},{17,25},{25,17},{2,10},{10... | collective-permute-start | bytes 786440 | tf_op jit(solution)/shard_map/ppermute | solution.py:156
  11.6 19.5 %collective-permute-start.1 = (f32[512,256]{1,0:T(8,128)S(1)}, f32[512,256]{1,0:T(8,128)S(1)}, u32[]{:S(2)}, u32[]{:S(2)}) collective-permute-start(f32[512,256]{1,0:T(8,128)S(1)} %maximum_select_fusion.vecs_ref), channel_id=1, source_target_pairs={{0,16},{8,24},{16,0},{24,8},{1,17},{9,25},{17,1},{25,9},{2,18},{10... | collective-permute-start | bytes 1572872 | tf_op jit(solution)/shard_map/ppermute | solution.py:156
  49.3 1.6 %copy-start = (f32[2048,256]{1,0:T(8,128)S(1)}, f32[2048,256]{1,0:T(8,128)}, u32[]{:S(2)}) copy-start(f32[2048,256]{1,0:T(8,128)} %all-gather.2.cloned.1.call-done.vecs_ref) | copy-start | bytes 6291460
  68.5 17.7 %collective-permute-start.2 = (f32[512,256]{1,0:T(8,128)S(1)}, f32[512,256]{1,0:T(8,128)S(1)}, u32[]{:S(2)}, u32[]{:S(2)}) collective-permute-start(f32[512,256]{1,0:T(8,128)S(1)} %left_terms.3), channel_id=1, source_target_pairs={{0,16},{8,24},{16,0},{24,8},{1,17},{9,25},{17,1},{25,9},{2,18},{10... | collective-permute-start | bytes 1572872 | tf_op jit(solution)/shard_map/ppermute | solution.py:156
  86.3 1.6 %collective-permute-start.3 = (f32[256,256]{1,0:T(8,128)S(1)}, f32[256,256]{1,0:T(8,128)S(1)}, u32[]{:S(2)}, u32[]{:S(2)}) collective-permute-start(f32[256,256]{1,0:T(8,128)S(1)} %dynamic-slice_add_fusion), channel_id=1, source_target_pairs={{0,8},{8,0},{16,24},{24,16},{1,9},{9,1},{17,25},{25,17},{2,10},{10... | collective-permute-start | bytes 786440 | tf_op jit(solution)/shard_map/ppermute | solution.py:156
Sparse Core Ops, SparseCore 0:
  9.5 36.0 all-gather.1
  49.3 33.2 reduce-scatter.1

commit v3 on v2

v3 whole, which is shorter than its diff:
```python
import functools
import jax
import jax.numpy as jnp
from jax import lax
from jax.experimental import pallas as pl
from jax.experimental.pallas import tpu as pltpu
from jax.sharding import PartitionSpec as P

LANES = 128
SLOTS = 3
VMEM_LIMIT = 48 * 2**20

epsilon = 1e-06


def fill_weights(lambdas_ref, weights):
    lambdas = lambdas_ref[...]
    terms = [jnp.ones_like(lambdas), lambdas]
    while len(terms) < weights.shape[0]:
        terms.append(2.0 * lambdas * terms[-1] - terms[-2])
    for term in range(weights.shape[0]):
        weights[term : term + 1, :] = terms[term]


def ring_order(count):
    return list(range(0, count, 2)) + list(range(1, count, 2))[::-1]


def halves(values):
    high = values.astype(jnp.bfloat16)
    return high, (values - high.astype(jnp.float32)).astype(jnp.bfloat16)


def product(left, right, dims):
    def dot(a, b):
        return lax.dot_general(a, b, (dims, ((), ())), preferred_element_type=jnp.float32)

    (left_high, left_low), (right_high, right_low) = left, right
    return dot(left_high, right_high) + dot(left_high, right_low) + dot(left_low, right_high)


def visit_matrices(matrices_ref, place, buffer, sem, piece_sem, prepare, work_piece, work):
    count, rows, _ = matrices_ref.shape
    width = buffer.shape[2]
    columns = pl.ds(pl.multiple_of(place * width, width), width)
    pieces = piece_sem.shape[0]
    depth = rows // pieces

    def copy(term):
        slot = lax.rem(term, SLOTS)
        return pltpu.make_async_copy(matrices_ref.at[term, :, columns], buffer.at[slot], sem.at[slot])

    def copy_piece(piece):
        part = pl.ds(pl.multiple_of(piece * depth, depth), depth)
        return pltpu.make_async_copy(matrices_ref.at[0, part, columns], buffer.at[0, part], piece_sem.at[piece])

    for piece in range(pieces):
        copy_piece(jnp.int32(piece)).start()
    for term in range(1, min(SLOTS, count)):
        copy(jnp.int32(term)).start()
    prepare()

    def visit_piece(piece, carry):
        copy_piece(piece).wait()
        work_piece(piece, buffer[0, pl.ds(pl.multiple_of(piece * depth, depth), depth), :])
        return carry

    lax.fori_loop(0, pieces, visit_piece, 0)

    def visit(term, carry):
        copy(term).wait()
        ahead = term + SLOTS - 1

        @pl.when(ahead < count)
        def _():
            copy(ahead).start()

        work(term, buffer[lax.rem(term, SLOTS)])
        return carry

    lax.fori_loop(1, count, visit, 0)


def right_kernel(order, n_vecs, places_ref, matrices_ref, lambdas_ref, *rest):
    vecs_refs, total_refs = rest[:n_vecs], rest[n_vecs:-7]
    out_ref, high, low, weights, buffer, sem, piece_sem = rest[-7:]
    count, rows, _ = matrices_ref.shape
    chunk = rows // len(order)

    def prepare():
        fill_weights(lambdas_ref, weights)
        for at, vecs_ref in enumerate(vecs_refs):
            share = vecs_ref.shape[0]
            place = pl.ds(pl.multiple_of(places_ref[1 + at] * share, share), share)

            def weigh(term, carry):
                high[term, place], low[term, place] = halves(vecs_ref[...] * weights[pl.ds(term, 1), :])
                return carry

            lax.fori_loop(0, count, weigh, 0)
        out_ref[...] = total_refs[0][...] if total_refs else jnp.zeros_like(out_ref)

    def work_piece(piece, block):
        terms = product(halves(block), (high[0], low[0]), ((1,), (0,)))
        for part, at in enumerate((piece, len(order) - 1 - piece)):
            out_ref[pl.ds(pl.multiple_of(at * chunk, chunk), chunk), :] += terms[part * chunk : (part + 1) * chunk, :]

    def work(term, block):
        terms = product(halves(block), (high[term], low[term]), ((1,), (0,)))
        for at, member in enumerate(order):
            out_ref[at * chunk : (at + 1) * chunk, :] += terms[member * chunk : (member + 1) * chunk, :]

    visit_matrices(matrices_ref, places_ref[0], buffer, sem, piece_sem, prepare, work_piece, work)


def left_kernel(order, places_ref, matrices_ref, lambdas_ref, vecs_hbm, out_ref, vecs, weights, buffer, sem, piece_sem, vecs_sem):
    count, rows, _ = matrices_ref.shape
    chunk = rows // len(order)
    fetch = pltpu.make_async_copy(vecs_hbm, vecs, vecs_sem)
    fetch.start()

    def prepare():
        fill_weights(lambdas_ref, weights)
        out_ref[...] = jnp.zeros_like(out_ref)
        fetch.wait()

    def work_piece(piece, block):
        places = [pl.ds(pl.multiple_of(at * chunk, chunk), chunk) for at in (piece, len(order) - 1 - piece)]
        held = jnp.concatenate([vecs[place, :] for place in places], axis=0)
        out_ref[...] += product(halves(block), halves(held * weights[0:1, :]), ((0,), (0,)))

    def work(term, block):
        places = [order.index(member) for member in range(len(order))]
        held = jnp.concatenate([vecs[at * chunk : (at + 1) * chunk, :] for at in places], axis=0)
        weighted = halves(held * weights[pl.ds(term, 1), :])
        out_ref[...] += product(halves(block), weighted, ((0,), (0,)))

    visit_matrices(matrices_ref, places_ref[0], buffer, sem, piece_sem, prepare, work_piece, work)


VMEM = pl.BlockSpec(memory_space=pltpu.VMEM)
SMEM = pl.BlockSpec(memory_space=pltpu.SMEM)
ANY = pl.BlockSpec(memory_space=pl.ANY)
HBM = pl.BlockSpec(memory_space=pltpu.HBM)


def cost(count, rows, width, trip):
    return pl.CostEstimate(
        flops=6 * count * rows * width * trip, bytes_accessed=4 * count * rows * width, transcendentals=0
    )


def right_terms(order, matrices, lambdas, vecs, places, total=()):
    count, rows, _ = matrices.shape
    trip = lambdas.shape[1]
    width = sum(part.shape[0] for part in vecs)
    pieces = len(order) // 2
    return pl.pallas_call(
        functools.partial(right_kernel, order, len(vecs)),
        out_shape=jax.ShapeDtypeStruct((rows, trip), jnp.float32),
        in_specs=[SMEM, ANY, VMEM] + [VMEM] * (len(vecs) + len(total)),
        out_specs=VMEM,
        scratch_shapes=[
            pltpu.VMEM((count, width, trip), jnp.bfloat16),
            pltpu.VMEM((count, width, trip), jnp.bfloat16),
            pltpu.VMEM((count, trip), jnp.float32),
            pltpu.VMEM((SLOTS, rows, width), jnp.float32),
            pltpu.SemaphoreType.DMA((SLOTS,)),
            pltpu.SemaphoreType.DMA((pieces,)),
        ],
        compiler_params=pltpu.CompilerParams(vmem_limit_bytes=VMEM_LIMIT),
        cost_estimate=cost(count, rows, width, trip),
        name="right_terms",
    )(jnp.stack(places), matrices, lambdas, *vecs, *total)


def left_terms(order, matrices, lambdas, vecs, place, width):
    count, rows, _ = matrices.shape
    trip = vecs.shape[1]
    pieces = len(order) // 2
    return pl.pallas_call(
        functools.partial(left_kernel, order),
        out_shape=jax.ShapeDtypeStruct((width, trip), jnp.float32),
        in_specs=[SMEM, ANY, VMEM, HBM],
        out_specs=VMEM,
        scratch_shapes=[
            pltpu.VMEM((rows, trip), jnp.float32),
            pltpu.VMEM((count, trip), jnp.float32),
            pltpu.VMEM((SLOTS, rows, width), jnp.float32),
            pltpu.SemaphoreType.DMA((SLOTS,)),
            pltpu.SemaphoreType.DMA((pieces,)),
            pltpu.SemaphoreType.DMA,
        ],
        compiler_params=pltpu.CompilerParams(vmem_limit_bytes=VMEM_LIMIT),
        cost_estimate=cost(count, rows, width, trip),
        name="left_terms",
    )(jnp.stack([place]), matrices, lambdas, vecs)


def exchange(values, axis, size, bit):
    return lax.ppermute(values, axis, [(i, i ^ bit) for i in range(size)])


def squares(values):
    return jnp.sum(values * values, axis=0)


def body(n_row, n_col, coefficients, lambdas, right_vecs, left_vecs):
    order = ring_order(n_col)
    lambdas = lambdas[None]
    share = right_vecs.shape[0]
    pair = 2 * share
    left_rows = lax.all_gather(left_vecs, "col", axis=0, tiled=True, axis_index_groups=[order])

    row = lax.axis_index("row").astype(jnp.int32)
    core = lax.rem(row, 2)
    in_pairs = n_row == 4 and pair % LANES == 0
    if in_pairs:
        here, there = row // 2, 1 - row // 2
        other = exchange(right_vecs, "row", n_row, 1)
        far = [exchange(right_vecs, "row", n_row, bit) for bit in (2, 3)]
        places = [core, 1 - core]
        right = right_terms(order, coefficients, lambdas, [right_vecs, other], [here] + places)
        right = right_terms(order, coefficients, lambdas, far, [there] + places, [right])
    else:
        right_cols = lax.all_gather(right_vecs, "row", axis=0, tiled=True)
        right = right_terms(order, coefficients, lambdas, [right_cols], [jnp.int32(0)] * 2)
    right_resid = lax.psum_scatter(right, "col", scatter_dimension=0, tiled=True, axis_index_groups=[order])
    right_squares = squares(right_resid)

    if in_pairs:
        sent = left_terms(order, coefficients, lambdas, left_rows, there, pair)
        came = exchange(sent, "row", n_row, 2)
        kept = left_terms(order, coefficients, lambdas, left_rows, here, pair)

        def part(values, which):
            return lax.dynamic_slice_in_dim(values, which * share, share, 0)

        last = exchange(part(kept, 1 - core) + part(came, 1 - core), "row", n_row, 1)
        last, right_squares = lax.optimization_barrier((last, right_squares))
        left_resid = part(kept, core) + part(came, core) + last
    else:
        left = left_terms(order, coefficients, lambdas, left_rows, jnp.int32(0), n_row * share)
        left_resid = lax.psum_scatter(left, "row", scatter_dimension=0, tiled=True)

    sums = jnp.stack([right_squares, squares(left_resid)])
    devices = n_row * n_col
    copies = jnp.broadcast_to(sums[None], (devices,) + sums.shape)
    parts = lax.all_to_all(copies, ("row", "col"), split_axis=0, concat_axis=0, tiled=True)
    rows = coefficients.shape[1] * n_row
    root_mean = jnp.sqrt(jnp.sum(parts, axis=0) / rows + epsilon)
    return (right_resid, left_resid, root_mean)


def solution(mesh):
    return jax.shard_map(
        functools.partial(body, mesh.shape["row"], mesh.shape["col"]),
        mesh=mesh,
        in_specs=(P(None, "row", "col"), P(), P(("col", "row"), None), P(("row", "col"), None)),
        out_specs=(P(("row", "col"), None), P(("col", "row"), None), P()),
        check_vma=False,
    )
```

time: 111 us -> 114 us (1.027)
  Pallas kernels: 70.2 us -> 75 us
  other arithmetic: 4.91 us -> 2.6 us
  starting transfers between devices: 3.57 us -> 5.18 us
  local copies, waits for them, and re-layouts: 2.31 us -> 3.87 us
  blocking collectives: 13.5 us -> 12 us
    pallas_call x2, Pallas kernels: 35 us -> 37.4 us  [right_terms(): pl.pallas_call(functools.partial(right_kernel, order, len(vecs)), out_sha...]
    pallas_call x2, Pallas kernels: 35.2 us -> 37.6 us  [left_terms(): pl.pallas_call(functools.partial(left_kernel, order), out_shape=jax.Shape...]
    unnamed x2 -> x10, local copies, waits for them, and re-layouts: 1.58 us -> 3.85 us
    ppermute x4 -> x5, starting transfers between devices: 3.49 us -> 5.11 us  [exchange(): return lax.ppermute(values, axis, [(i, i ^ bit) for i in range(size)])]
    all_to_all x1, blocking collectives: 13.5 us -> 12 us  [body(): lax.all_to_all(copies, ('row', 'col'), split_axis=0, concat_axis=0, tiled...]
    sub x2 -> x0, other arithmetic: 1.38 us -> none  [chebyshev(): terms.append(2.0 * lambdas * terms[-1] - terms[-2])]
  transfers between devices with their start and end apart: 6 -> 7, of which waited for: 1 -> 1; matrix products, arithmetic and copies ran while one was open for 4% -> 1% of each run, Pallas kernels for 63% -> 66%
where the time goes in v3:
time: 114 us
  Pallas kernels  75 us (66%)
  between operations  14.1 us (12%)
  blocking collectives  12 us (11%)
  starting transfers between devices  5.18 us (5%)
  local copies, waits for them, and re-layouts  3.87 us (3%)
  other arithmetic  2.6 us (2%)
  waiting for transfers between devices  1.17 us (1%)
    pallas_call x2, Pallas kernels, left_terms(): pl.pallas_call(functools.partial(left_kernel, order), out_shape=jax.Shape...  37.6 us
    pallas_call x2, Pallas kernels, right_terms(): pl.pallas_call(functools.partial(right_kernel, order, len(vecs)), out_sha...  37.4 us
    all_to_all x1, blocking collectives, body(): lax.all_to_all(copies, ('row', 'col'), split_axis=0, concat_axis=0, tiled...  12 us
    ppermute x5, starting transfers between devices, exchange(): return lax.ppermute(values, axis, [(i, i ^ bit) for i in range(size)])  5.11 us
    unnamed x10, local copies, waits for them, and re-layouts  3.85 us
  transfers between devices with their start and end apart: 7, of which 1 were waited for; matrix products, arithmetic and copies ran while one was open for 1% of the time, Pallas kernels for 66%

profile of v3, /device:TPU:0, one launch (start us, length us, event | category | flops | bytes accessed | tf_op | source)
XLA Modules:
  0.0 114.0 jit_solution(17797134464548426716)
XLA Ops:
  7.2 0.0 all-gather.2.cloned.1.call-start
  7.2 0.7 all-gather.2.cloned.1.call-update
  7.9 0.0 reduce-scatter.2.cloned.1.call-start
  7.9 0.5 collective-permute-start.2
  8.5 2.6 %collective-permute-start = (f32[256,256]{1,0:T(8,128)}, f32[256,256]{1,0:T(8,128)S(1)}, u32[]{:S(2)}, u32[]{:S(2)}) collective-permute-start(f32[256,256]{1,0:T(8,128)} %rest_0_.1), channel_id=1, source_target_pairs={{0,16},{8,24},{16,0},{24,8},{1,17},{9,25},{17,1},{25,9},{2,18},{10... | collective-permute-start | bytes 786440 | tf_op jit(solution)/shard_map/ppermute | solution.py:201
  11.0 0.1 collective-permute-start.1
  11.1 0.1 add_add_fusion.2.places_ref
  11.2 0.1 add_add_fusion.1.places_ref
  11.2 0.0 collective-permute-done.2.rest_1_
  11.3 0.0 copy-start.2
  11.3 1.0 copy-done.2
  12.2 0.7 copy-done.3
  12.9 18.2 %right_terms.2.rest_2_ = f32[2048,256]{1,0:T(8,128)S(1)} custom-call(s32[3]{0:T(128)S(1)} %add_add_fusion.2.places_ref, f32[8,2048,1024]{2,1,0:T(8,128)} %matrices_ref.7, f32[1,256]{1,0:T(1,128)S(1)} %bitcast.7, f32[256,256]{1,0:T(8,128)S(1)} %copy-done.2, f32[256,256]{1,0:T(8,128)S(1)} %collective-permute-done.2.rest_1_), custom_call_target="tpu_custom_call" | custom-call | flops 12884901888 | bytes 33554432 | tf_op jit(solution)/shard_map/right_terms/pallas_call | solution.py:158
  31.1 0.0 collective-permute-done.rest_0_
  31.1 0.0 collective-permute-done.1.rest_1_
  31.1 19.2 %right_terms.3 = f32[2048,256]{1,0:T(8,128)} custom-call(s32[3]{0:T(128)S(1)} %add_add_fusion.1.places_ref, f32[8,2048,1024]{2,1,0:T(8,128)} %matrices_ref.7, f32[1,256]{1,0:T(1,128)S(1)} %bitcast.8, f32[256,256]{1,0:T(8,128)S(1)} %collective-permute-done.rest_0_, f32[256,256]{1,0:T(8,128)S(1)} %collective-permute-done.1.rest_1_, ...), custom_call_target="tpu_custom_call" | custom-call | flops 12884901888 | bytes 33554432 | tf_op jit(solution)/shard_map/right_terms/pallas_call | solution.py:158
  50.3 0.0 copy-start.4
  50.3 0.0 reduce-scatter.2.cloned.1.call-update
  50.3 0.0 all-gather.2.cloned.1.call-done.vecs_hbm
  50.4 0.6 copy-done.4
  51.0 1.6 %copy-done = f32[2048,256]{1,0:T(8,128)S(1)} copy-done((f32[2048,256]{1,0:T(8,128)S(1)}, f32[2048,256]{1,0:T(8,128)}, u32[]{:S(2)}) %copy-start) | copy-done | bytes 2097176
  52.6 18.9 %left_terms.3 = f32[512,256]{1,0:T(8,128)S(1)} custom-call(s32[1]{0:T(128)} %bitcast.places_ref, f32[8,2048,1024]{2,1,0:T(8,128)} %matrices_ref.7, f32[1,256]{1,0:T(1,128)S(1)} %bitcast.9, f32[2048,256]{1,0:T(8,128)S(1)} %copy-done), custom_call_target="tpu_custom_call" | custom-call | flops 12884901888 | bytes 33554432 | tf_op jit(solution)/shard_map/left_terms/pallas_call | solution.py:181
  71.5 1.8 %collective-permute-start.3 = (f32[512,256]{1,0:T(8,128)S(1)}, f32[512,256]{1,0:T(8,128)S(1)}, u32[]{:S(2)}, u32[]{:S(2)}) collective-permute-start(f32[512,256]{1,0:T(8,128)S(1)} %left_terms.3), channel_id=1, source_target_pairs={{0,16},{8,24},{16,0},{24,8},{1,17},{9,25},{17,1},{25,9},{2,18},{10... | collective-permute-start | bytes 1572872 | tf_op jit(solution)/shard_map/ppermute | solution.py:201
  73.3 0.0 copy-done.1
  73.3 18.8 %left_terms.2 = f32[512,256]{1,0:T(8,128)S(1)} custom-call(s32[1]{0:T(128)} %bitcast.4.places_ref, f32[8,2048,1024]{2,1,0:T(8,128)} %matrices_ref.7, f32[1,256]{1,0:T(1,128)S(1)} %bitcast.10, f32[2048,256]{1,0:T(8,128)S(1)} %copy-done.1), custom_call_target="tpu_custom_call" | custom-call | flops 12884901888 | bytes 33554432 | tf_op jit(solution)/shard_map/left_terms/pallas_call | solution.py:181
  92.0 0.0 collective-permute-done.3
  92.1 0.2 collective-permute-start.4
  92.3 1.0 multiply_reduce_fusion.1
  93.3 0.4 collective-permute-done.4
  93.7 0.8 multiply_reduce_fusion
  94.5 12.0 %all_to_all.5 = f32[32,2,256]{2,1,0:T(2,128)S(1)} all-to-all(f32[32,2,256]{2,1,0:T(2,128)S(1)} %broadcast_in_dim.10), channel_id=1, replica_groups=mesh['row'=4,'col'=8] {'row','col'}, dimensions={0} | all-to-all | bytes 131072 | tf_op jit(solution)/shard_map/all_to_all | solution.py:249
  106.6 0.6 add_sqrt_fusion
  (8 shorter events, 0.1 us)
Async XLA Ops:
  7.2 43.2 %all-gather.2.cloned.1.call-start = ((), (), s32[]{:S(2)}) async-start(), calls=%async_computation.3 | async-start | bytes 2359296 | tf_op jit(solution)/shard_map/all_gather | solution.py:213
  7.9 84.4 %reduce-scatter.2.cloned.1.call-start = ((), (), s32[]{:S(2)}) async-start(), calls=%async_computation.2 | async-start | bytes 2359296 | tf_op jit(solution)/shard_map/reduce_scatter | solution.py:228
  7.9 3.3 %collective-permute-start.2 = (f32[256,256]{1,0:T(8,128)}, f32[256,256]{1,0:T(8,128)S(1)}, u32[]{:S(2)}, u32[]{:S(2)}) collective-permute-start(f32[256,256]{1,0:T(8,128)} %rest_0_.1), channel_id=1, source_target_pairs={{0,8},{8,0},{16,24},{24,16},{1,9},{9,1},{17,25},{25,17},{2,10},{10... | collective-permute-start | bytes 786440 | tf_op jit(solution)/shard_map/ppermute | solution.py:201
  8.5 22.6 %collective-permute-start = (f32[256,256]{1,0:T(8,128)}, f32[256,256]{1,0:T(8,128)S(1)}, u32[]{:S(2)}, u32[]{:S(2)}) collective-permute-start(f32[256,256]{1,0:T(8,128)} %rest_0_.1), channel_id=1, source_target_pairs={{0,16},{8,24},{16,0},{24,8},{1,17},{9,25},{17,1},{25,9},{2,18},{10... | collective-permute-start | bytes 786440 | tf_op jit(solution)/shard_map/ppermute | solution.py:201
  11.0 20.1 %collective-permute-start.1 = (f32[256,256]{1,0:T(8,128)}, f32[256,256]{1,0:T(8,128)S(1)}, u32[]{:S(2)}, u32[]{:S(2)}) collective-permute-start(f32[256,256]{1,0:T(8,128)} %rest_0_.1), channel_id=1, source_target_pairs={{0,24},{8,16},{16,8},{24,0},{1,25},{9,17},{17,9},{25,1},{2,26},{10... | collective-permute-start | bytes 786440 | tf_op jit(solution)/shard_map/ppermute | solution.py:201
  11.3 1.0 copy-start.2
  12.2 0.7 copy-start.3
  50.3 0.7 copy-start.4
  51.0 1.6 %copy-start = (f32[2048,256]{1,0:T(8,128)S(1)}, f32[2048,256]{1,0:T(8,128)}, u32[]{:S(2)}) copy-start(f32[2048,256]{1,0:T(8,128)} %all-gather.2.cloned.1.call-done.vecs_hbm) | copy-start | bytes 6291460
  52.6 20.7 %copy-start.1 = (f32[2048,256]{1,0:T(8,128)S(1)}, f32[2048,256]{1,0:T(8,128)}, u32[]{:S(2)}) copy-start(f32[2048,256]{1,0:T(8,128)} %all-gather.2.cloned.1.call-done.vecs_hbm) | copy-start | bytes 6291460
  71.5 20.6 %collective-permute-start.3 = (f32[512,256]{1,0:T(8,128)S(1)}, f32[512,256]{1,0:T(8,128)S(1)}, u32[]{:S(2)}, u32[]{:S(2)}) collective-permute-start(f32[512,256]{1,0:T(8,128)S(1)} %left_terms.3), channel_id=1, source_target_pairs={{0,16},{8,24},{16,0},{24,8},{1,17},{9,25},{17,1},{25,9},{2,18},{10... | collective-permute-start | bytes 1572872 | tf_op jit(solution)/shard_map/ppermute | solution.py:201
  92.1 1.6 %collective-permute-start.4 = (f32[256,256]{1,0:T(8,128)S(1)}, f32[256,256]{1,0:T(8,128)S(1)}, u32[]{:S(2)}, u32[]{:S(2)}) collective-permute-start(f32[256,256]{1,0:T(8,128)S(1)} %dynamic-slice_add_fusion), channel_id=1, source_target_pairs={{0,8},{8,0},{16,24},{24,16},{1,9},{9,1},{17,25},{25,17},{2,10},{10... | collective-permute-start | bytes 786440 | tf_op jit(solution)/shard_map/ppermute | solution.py:201
Sparse Core Ops, SparseCore 0:
  9.5 36.0 all-gather.1
  50.5 34.4 reduce-scatter.1

commit v4 on v2

--- a/solution.py
+++ b/solution.py
@@ -48,7 +48,7 @@
     return copy
 
 
-def each_matrix(count, copy, step):
+def each_matrix(first, count, copy, step):
     def visit(term, carry):
         copy(term).wait()
         ahead = term + SLOTS - 1
@@ -60,15 +60,25 @@
         step(term)
         return carry
 
-    lax.fori_loop(0, count, visit, 0)
+    lax.fori_loop(first, count, visit, 0)
 
 
 def right_kernel(order, has_total, place_ref, matrices_ref, vecs_ref, weights_ref, *rest):
-    out_ref, high, low, buffer, sem = rest[-5:]
+    out_ref, high, low, buffer, sem, piece_sem = rest[-6:]
     count, rows, _ = matrices_ref.shape
     chunk = rows // len(order)
     copy = block_copies(matrices_ref, place_ref[0], buffer, sem)
-    for term in range(min(SLOTS, count)):
+    depth = 2 * chunk
+    width = buffer.shape[2]
+    columns = pl.ds(pl.multiple_of(place_ref[0] * width, width), width)
+
+    def copy_piece(piece):
+        part = pl.ds(pl.multiple_of(piece * depth, depth), depth)
+        return pltpu.make_async_copy(matrices_ref.at[0, part, columns], buffer.at[0, part], piece_sem.at[piece])
+
+    for piece in range(rows // depth):
+        copy_piece(jnp.int32(piece)).start()
+    for term in range(1, min(SLOTS, count)):
         copy(jnp.int32(term)).start()
     out_ref[...] = rest[0][...] if has_total else jnp.zeros_like(out_ref)
 
@@ -77,13 +87,23 @@
         return carry
 
     lax.fori_loop(0, count, weigh, 0)
+
+    def step_piece(piece, carry):
+        copy_piece(piece).wait()
+        block = buffer[0, pl.ds(pl.multiple_of(piece * depth, depth), depth), :]
+        terms = product(halves(block), (high[0], low[0]), ((1,), (0,)))
+        for part, at in enumerate((piece, len(order) - 1 - piece)):
+            out_ref[pl.ds(pl.multiple_of(at * chunk, chunk), chunk), :] += terms[part * chunk : (part + 1) * chunk, :]
+        return carry
+
+    lax.fori_loop(0, rows // depth, step_piece, 0)
 
     def step(term):
         terms = product(halves(buffer[lax.rem(term, SLOTS)]), (high[term], low[term]), ((1,), (0,)))
         for at, member in enumerate(order):
             out_ref[at * chunk : (at + 1) * chunk, :] += terms[member * chunk : (member + 1) * chunk, :]
 
-    each_matrix(count, copy, step)
+    each_matrix(1, count, copy, step)
 
 
 def left_kernel(order, place_ref, matrices_ref, vecs_ref, weights_ref, out_ref, buffer, sem):
@@ -100,7 +120,7 @@
         weighted = halves(vecs * weights_ref[pl.ds(term, 1), :])
         out_ref[...] += product(halves(buffer[lax.rem(term, SLOTS)]), weighted, ((0,), (0,)))
 
-    each_matrix(count, copy, step)
+    each_matrix(0, count, copy, step)
 
 
 VMEM = pl.BlockSpec(memory_space=pltpu.VMEM)
@@ -127,6 +147,7 @@
             pltpu.VMEM((count, width, trip), jnp.bfloat16),
             pltpu.VMEM((SLOTS, rows, width), jnp.float32),
             pltpu.SemaphoreType.DMA((SLOTS,)),
+            pltpu.SemaphoreType.DMA((len(order) // 2,)),
         ],
         compiler_params=pltpu.CompilerParams(vmem_limit_bytes=VMEM_LIMIT),
         cost_estimate=cost(count, rows, width, trip),
@@ -181,6 +202,7 @@
         right_cols = lax.all_gather(right_vecs, "row", axis=0, tiled=True)
         right = right_terms(order, coefficients, right_cols, weights, jnp.int32(0))
     right_resid = lax.psum_scatter(right, "col", scatter_dimension=0, tiled=True, axis_index_groups=[order])
+    right_squares = squares(right_resid)
 
     if n_row == 4 and pair % LANES == 0:
         sent = left_terms(order, coefficients, left_rows, weights, there, pair)
@@ -191,12 +213,13 @@
             return lax.dynamic_slice_in_dim(values, which * share, share, 0)
 
         other = part(kept, 1 - core) + part(came, 1 - core)
-        left_resid = part(kept, core) + part(came, core) + exchange(other, "row", n_row, 1)
+        last, right_squares = lax.optimization_barrier((exchange(other, "row", n_row, 1), right_squares))
+        left_resid = part(kept, core) + part(came, core) + last
     else:
         left = left_terms(order, coefficients, left_rows, weights, jnp.int32(0), n_row * share)
         left_resid = lax.psum_scatter(left, "row", scatter_dimension=0, tiled=True)
 
-    sums = jnp.stack([squares(right_resid), squares(left_resid)])
+    sums = jnp.stack([right_squares, squares(left_resid)])
     devices = n_row * n_col
     copies = jnp.broadcast_to(sums[None], (devices,) + sums.shape)
     parts = lax.all_to_all(copies, ("row", "col"), split_axis=0, concat_axis=0, tiled=True)

time: 111 us -> 109 us (0.982)
  transfers between devices with their start and end apart: 6 -> 6, of which waited for: 1 -> 1; matrix products, arithmetic and copies ran while one was open for 4% -> 4% of each run, Pallas kernels for 63% -> 64%
where the time goes in v4:
time: 109 us
  Pallas kernels  69.3 us (64%)
  between operations  14.1 us (13%)
  blocking collectives  13.4 us (12%)
  other arithmetic  4.91 us (5%)
  starting transfers between devices  3.58 us (3%)
  local copies, waits for them, and re-layouts  2.31 us (2%)
    pallas_call x2, Pallas kernels, left_terms(): pl.pallas_call(functools.partial(left_kernel, order), out_shape=jax.Shape...  35.2 us
    pallas_call x2, Pallas kernels, right_terms(): pl.pallas_call(functools.partial(right_kernel, order, total is not None),...  34 us
    all_to_all x1, blocking collectives, body(): lax.all_to_all(copies, ('row', 'col'), split_axis=0, concat_axis=0, tiled...  13.4 us
    ppermute x4, starting transfers between devices, exchange(): return lax.ppermute(values, axis, [(i, i ^ bit) for i in range(size)])  3.5 us
  transfers between devices with their start and end apart: 6, of which 1 were waited for; matrix products, arithmetic and copies ran while one was open for 4% of the time, Pallas kernels for 64%

profile of v4, /device:TPU:0, one launch (start us, length us, event | category | flops | bytes accessed | tf_op | source)
XLA Modules:
  0.0 108.7 jit_solution(16125287047543820956)
XLA Ops:
  7.2 0.0 all-gather.2.cloned.1.call-start
  7.2 0.7 all-gather.2.cloned.1.call-update
  7.9 0.0 reduce-scatter.2.cloned.1.call-start
  7.9 0.5 collective-permute-start
  8.5 0.7 multiply_subtract_fusion
  9.2 0.7 multiply_subtract_fusion.1
  9.8 0.7 stack.40.weights_ref
  10.6 0.0 collective-permute-done
  10.6 1.1 maximum_select_fusion.vecs_ref
  11.6 2.6 %collective-permute-start.1 = (f32[512,256]{1,0:T(8,128)S(1)}, f32[512,256]{1,0:T(8,128)S(1)}, u32[]{:S(2)}, u32[]{:S(2)}) collective-permute-start(f32[512,256]{1,0:T(8,128)S(1)} %maximum_select_fusion.vecs_ref), channel_id=1, source_target_pairs={{0,16},{8,24},{16,0},{24,8},{1,17},{9,25},{17,1},{25,9},{2,18},{10... | collective-permute-start | bytes 1572872 | tf_op jit(solution)/shard_map/ppermute | solution.py:177
  14.2 16.4 %right_terms.2.rest_0_ = f32[2048,256]{1,0:T(8,128)S(1)} custom-call(s32[1]{0:T(128)} %bitcast.8.place_ref, f32[8,2048,1024]{2,1,0:T(8,128)} %matrices_ref.7, f32[512,256]{1,0:T(8,128)S(1)} %maximum_select_fusion.vecs_ref, f32[8,256]{1,0:T(8,128)S(1)} %stack.40.weights_ref), custom_call_target="tpu_custom_call" | custom-call | flops 12884901888 | bytes 33554432 | tf_op jit(solution)/shard_map/right_terms/pallas_call | solution.py:140
  30.7 0.0 collective-permute-done.1.vecs_ref
  30.7 17.6 %right_terms.3 = f32[2048,256]{1,0:T(8,128)} custom-call(s32[1]{0:T(128)} %bitcast.place_ref, f32[8,2048,1024]{2,1,0:T(8,128)} %matrices_ref.7, f32[512,256]{1,0:T(8,128)S(1)} %collective-permute-done.1.vecs_ref, f32[8,256]{1,0:T(8,128)S(1)} %stack.40.weights_ref, f32[2048,256]{1,0:T(8,128)S(1)} %right_terms.2.rest_0_), custom_call_target="tpu_custom_call" | custom-call | flops 12884901888 | bytes 33554432 | tf_op jit(solution)/shard_map/right_terms/pallas_call | solution.py:140
  48.3 0.0 reduce-scatter.2.cloned.1.call-update
  48.3 0.0 all-gather.2.cloned.1.call-done.vecs_ref
  48.3 0.0 copy-start
  48.4 1.6 %copy-done = f32[2048,256]{1,0:T(8,128)S(1)} copy-done((f32[2048,256]{1,0:T(8,128)S(1)}, f32[2048,256]{1,0:T(8,128)}, u32[]{:S(2)}) %copy-start) | copy-done | bytes 2097176
  49.9 17.6 %left_terms.3 = f32[512,256]{1,0:T(8,128)S(1)} custom-call(s32[1]{0:T(128)} %bitcast.place_ref, f32[8,2048,1024]{2,1,0:T(8,128)} %matrices_ref.7, f32[2048,256]{1,0:T(8,128)S(1)} %copy-done, f32[8,256]{1,0:T(8,128)S(1)} %stack.40.weights_ref), custom_call_target="tpu_custom_call" | custom-call | flops 12884901888 | bytes 33554432 | tf_op jit(solution)/shard_map/left_terms/pallas_call | solution.py:161
  67.5 0.1 collective-permute-start.2
  67.7 17.6 %left_terms.2 = f32[512,256]{1,0:T(8,128)S(1)} custom-call(s32[1]{0:T(128)} %bitcast.8.place_ref, f32[8,2048,1024]{2,1,0:T(8,128)} %matrices_ref.7, f32[2048,256]{1,0:T(8,128)S(1)} %copy-done, f32[8,256]{1,0:T(8,128)S(1)} %stack.40.weights_ref), custom_call_target="tpu_custom_call" | custom-call | flops 12884901888 | bytes 33554432 | tf_op jit(solution)/shard_map/left_terms/pallas_call | solution.py:161
  85.3 0.0 collective-permute-done.2
  85.4 0.3 collective-permute-start.3
  85.7 0.0 reduce-scatter.2.cloned.1.call-done
  85.7 1.0 multiply_reduce_fusion.1
  86.7 0.3 collective-permute-done.3
  87.0 0.8 multiply_reduce_fusion
  87.7 13.4 %all_to_all.5 = f32[32,2,256]{2,1,0:T(2,128)S(1)} all-to-all(f32[32,2,256]{2,1,0:T(2,128)S(1)} %broadcast_in_dim.2), channel_id=1, replica_groups=mesh['row'=4,'col'=8] {'row','col'}, dimensions={0} | all-to-all | bytes 131072 | tf_op jit(solution)/shard_map/all_to_all | solution.py:225
  101.2 0.6 add_sqrt_fusion
  (5 shorter events, 0.1 us)
Async XLA Ops:
  7.2 41.2 %all-gather.2.cloned.1.call-start = ((), (), s32[]{:S(2)}) async-start(), calls=%async_computation.3 | async-start | bytes 2359296 | tf_op jit(solution)/shard_map/all_gather | solution.py:189
  7.9 77.8 %reduce-scatter.2.cloned.1.call-start = ((), (), s32[]{:S(2)}) async-start(), calls=%async_computation.2 | async-start | bytes 2359296 | tf_op jit(solution)/shard_map/reduce_scatter | solution.py:204
  7.9 2.6 %collective-permute-start = (f32[256,256]{1,0:T(8,128)}, f32[256,256]{1,0:T(8,128)S(1)}, u32[]{:S(2)}, u32[]{:S(2)}) collective-permute-start(f32[256,256]{1,0:T(8,128)} %param.6), channel_id=1, source_target_pairs={{0,8},{8,0},{16,24},{24,16},{1,9},{9,1},{17,25},{25,17},{2,10},{10... | collective-permute-start | bytes 786440 | tf_op jit(solution)/shard_map/ppermute | solution.py:177
  11.6 19.0 %collective-permute-start.1 = (f32[512,256]{1,0:T(8,128)S(1)}, f32[512,256]{1,0:T(8,128)S(1)}, u32[]{:S(2)}, u32[]{:S(2)}) collective-permute-start(f32[512,256]{1,0:T(8,128)S(1)} %maximum_select_fusion.vecs_ref), channel_id=1, source_target_pairs={{0,16},{8,24},{16,0},{24,8},{1,17},{9,25},{17,1},{25,9},{2,18},{10... | collective-permute-start | bytes 1572872 | tf_op jit(solution)/shard_map/ppermute | solution.py:177
  48.3 1.6 %copy-start = (f32[2048,256]{1,0:T(8,128)S(1)}, f32[2048,256]{1,0:T(8,128)}, u32[]{:S(2)}) copy-start(f32[2048,256]{1,0:T(8,128)} %all-gather.2.cloned.1.call-done.vecs_ref) | copy-start | bytes 6291460
  67.5 17.8 %collective-permute-start.2 = (f32[512,256]{1,0:T(8,128)S(1)}, f32[512,256]{1,0:T(8,128)S(1)}, u32[]{:S(2)}, u32[]{:S(2)}) collective-permute-start(f32[512,256]{1,0:T(8,128)S(1)} %left_terms.3), channel_id=1, source_target_pairs={{0,16},{8,24},{16,0},{24,8},{1,17},{9,25},{17,1},{25,9},{2,18},{10... | collective-permute-start | bytes 1572872 | tf_op jit(solution)/shard_map/ppermute | solution.py:177
  85.4 1.6 %collective-permute-start.3 = (f32[256,256]{1,0:T(8,128)S(1)}, f32[256,256]{1,0:T(8,128)S(1)}, u32[]{:S(2)}, u32[]{:S(2)}) collective-permute-start(f32[256,256]{1,0:T(8,128)S(1)} %dynamic-slice_add_fusion), channel_id=1, source_target_pairs={{0,8},{8,0},{16,24},{24,16},{1,9},{9,1},{17,25},{25,17},{2,10},{10... | collective-permute-start | bytes 786440 | tf_op jit(solution)/shard_map/ppermute | solution.py:177
Sparse Core Ops, SparseCore 0:
  9.5 36.0 all-gather.1
  48.5 33.1 reduce-scatter.1

commit v5 on v4

--- a/solution.py
+++ b/solution.py
@@ -106,7 +106,7 @@
     each_matrix(1, count, copy, step)
 
 
-def left_kernel(order, place_ref, matrices_ref, vecs_ref, weights_ref, out_ref, buffer, sem):
+def left_kernel(order, place_ref, matrices_ref, high_ref, low_ref, weights_ref, out_ref, buffer, sem):
     count, rows, _ = matrices_ref.shape
     chunk = rows // len(order)
     copy = block_copies(matrices_ref, place_ref[0], buffer, sem)
@@ -116,9 +116,11 @@
     at = [order.index(member) for member in range(len(order))]
 
     def step(term):
-        vecs = jnp.concatenate([vecs_ref[i * chunk : (i + 1) * chunk, :] for i in at], axis=0)
-        weighted = halves(vecs * weights_ref[pl.ds(term, 1), :])
-        out_ref[...] += product(halves(buffer[lax.rem(term, SLOTS)]), weighted, ((0,), (0,)))
+        vecs = [
+            jnp.concatenate([ref[i * chunk : (i + 1) * chunk, :] for i in at], axis=0) for ref in (high_ref, low_ref)
+        ]
+        terms = product(halves(buffer[lax.rem(term, SLOTS)]), vecs, ((0,), (0,)))
+        out_ref[...] += terms * weights_ref[pl.ds(term, 1), :]
 
     each_matrix(0, count, copy, step)
 
@@ -157,11 +159,11 @@
 
 def left_terms(order, matrices, vecs, weights, place, width):
     count, rows, _ = matrices.shape
-    trip = vecs.shape[1]
+    trip = vecs[0].shape[1]
     return pl.pallas_call(
         functools.partial(left_kernel, order),
         out_shape=jax.ShapeDtypeStruct((width, trip), jnp.float32),
-        in_specs=[SMEM, ANY, VMEM, VMEM],
+        in_specs=[SMEM, ANY, VMEM, VMEM, VMEM],
         out_specs=VMEM,
         scratch_shapes=[
             pltpu.VMEM((SLOTS, rows, width), jnp.float32),
@@ -170,7 +172,7 @@
         compiler_params=pltpu.CompilerParams(vmem_limit_bytes=VMEM_LIMIT),
         cost_estimate=cost(count, rows, width, trip),
         name="left_terms",
-    )(jnp.reshape(place, (1,)), matrices, vecs, weights)
+    )(jnp.reshape(place, (1,)), matrices, *vecs, weights)
 
 
 def exchange(values, axis, size, bit):
@@ -187,6 +189,9 @@
     share = right_vecs.shape[0]
     pair = 2 * share
     left_rows = lax.all_gather(left_vecs, "col", axis=0, tiled=True, axis_index_groups=[order])
+
+    left_high = lax.reduce_precision(left_rows, 8, 7)
+    left_halves = (left_high.astype(jnp.bfloat16), (left_rows - left_high).astype(jnp.bfloat16))
 
     row = lax.axis_index("row").astype(jnp.int32)
     core = lax.rem(row, 2)
@@ -205,9 +210,9 @@
     right_squares = squares(right_resid)
 
     if n_row == 4 and pair % LANES == 0:
-        sent = left_terms(order, coefficients, left_rows, weights, there, pair)
+        sent = left_terms(order, coefficients, left_halves, weights, there, pair)
         came = exchange(sent, "row", n_row, 2)
-        kept = left_terms(order, coefficients, left_rows, weights, here, pair)
+        kept = left_terms(order, coefficients, left_halves, weights, here, pair)
 
         def part(values, which):
             return lax.dynamic_slice_in_dim(values, which * share, share, 0)
@@ -216,7 +221,7 @@
         last, right_squares = lax.optimization_barrier((exchange(other, "row", n_row, 1), right_squares))
         left_resid = part(kept, core) + part(came, core) + last
     else:
-        left = left_terms(order, coefficients, left_rows, weights, jnp.int32(0), n_row * share)
+        left = left_terms(order, coefficients, left_halves, weights, jnp.int32(0), n_row * share)
         left_resid = lax.psum_scatter(left, "row", scatter_dimension=0, tiled=True)
 
     sums = jnp.stack([right_squares, squares(left_resid)])

time: 109 us -> 108 us (level)
  other arithmetic: 4.91 us -> 6.82 us
  local copies, waits for them, and re-layouts: 2.31 us -> 0.73 us
    convert_element_type x0 -> x1, other arithmetic: none -> 1.91 us  [body(): (left_rows - left_high).astype(jnp.bfloat16)]
    unnamed x2 -> x0, local copies, waits for them, and re-layouts: 1.58 us -> none
  transfers between devices with their start and end apart: 6 -> 6, of which waited for: 1 -> 1; matrix products, arithmetic and copies ran while one was open for 4% -> 6% of each run, Pallas kernels for 64% -> 63%
where the time goes in v5:
time: 108 us
  Pallas kernels  68.6 us (64%)
  between operations  14.1 us (13%)
  blocking collectives  13.4 us (12%)
  other arithmetic  6.82 us (6%)
  starting transfers between devices  3.55 us (3%)
    pallas_call x2, Pallas kernels, left_terms(): pl.pallas_call(functools.partial(left_kernel, order), out_shape=jax.Shape...  34.5 us
    pallas_call x2, Pallas kernels, right_terms(): pl.pallas_call(functools.partial(right_kernel, order, total is not None),...  34 us
    all_to_all x1, blocking collectives, body(): lax.all_to_all(copies, ('row', 'col'), split_axis=0, concat_axis=0, tiled...  13.4 us
    ppermute x4, starting transfers between devices, exchange(): return lax.ppermute(values, axis, [(i, i ^ bit) for i in range(size)])  3.47 us
  transfers between devices with their start and end apart: 6, of which 1 were waited for; matrix products, arithmetic and copies ran while one was open for 6% of the time, Pallas kernels for 63%

profile of v5, /device:TPU:0, one launch (start us, length us, event | category | flops | bytes accessed | tf_op | source)
XLA Modules:
  0.0 108.2 jit_solution(10152925154586717425)
XLA Ops:
  7.2 0.0 all-gather.2.cloned.1.call-start
  7.2 0.7 all-gather.2.cloned.1.call-update
  7.9 0.0 reduce-scatter.2.cloned.1.call-start
  7.9 0.5 collective-permute-start
  8.5 0.7 multiply_subtract_fusion
  9.2 0.7 multiply_subtract_fusion.1
  9.8 0.7 stack.40.weights_ref
  10.6 0.0 collective-permute-done
  10.6 1.1 %maximum_select_fusion.vecs_ref = f32[512,256]{1,0:T(8,128)S(1)} fusion(f32[256,256]{1,0:T(8,128)S(1)} %collective-permute-done, f32[256,256]{1,0:T(8,128)} %param.6, pred[]{:T(512)S(6)} %eq.3), kind=kLoop, calls=%fused_computation.3 | loop fusion | flops 393216 | bytes 1048577 | tf_op jit(solution)/shard_map/jit(_where)/select_n | solution.py:202
  11.6 2.6 %collective-permute-start.1 = (f32[512,256]{1,0:T(8,128)S(1)}, f32[512,256]{1,0:T(8,128)S(1)}, u32[]{:S(2)}, u32[]{:S(2)}) collective-permute-start(f32[512,256]{1,0:T(8,128)S(1)} %maximum_select_fusion.vecs_ref), channel_id=1, source_target_pairs={{0,16},{8,24},{16,0},{24,8},{1,17},{9,25},{17,1},{25,9},{2,18},{10... | collective-permute-start | bytes 1572872 | tf_op jit(solution)/shard_map/ppermute | solution.py:179
  14.2 16.4 %right_terms.2.rest_0_ = f32[2048,256]{1,0:T(8,128)S(1)} custom-call(s32[1]{0:T(128)} %bitcast.8.place_ref, f32[8,2048,1024]{2,1,0:T(8,128)} %matrices_ref.7, f32[512,256]{1,0:T(8,128)S(1)} %maximum_select_fusion.vecs_ref, f32[8,256]{1,0:T(8,128)S(1)} %stack.40.weights_ref), custom_call_target="tpu_custom_call" | custom-call | flops 12884901888 | bytes 33554432 | tf_op jit(solution)/shard_map/right_terms/pallas_call | solution.py:142
  30.7 0.0 collective-permute-done.1.vecs_ref
  30.7 17.6 %right_terms.3 = f32[2048,256]{1,0:T(8,128)} custom-call(s32[1]{0:T(128)} %bitcast.place_ref, f32[8,2048,1024]{2,1,0:T(8,128)} %matrices_ref.7, f32[512,256]{1,0:T(8,128)S(1)} %collective-permute-done.1.vecs_ref, f32[8,256]{1,0:T(8,128)S(1)} %stack.40.weights_ref, f32[2048,256]{1,0:T(8,128)S(1)} %right_terms.2.rest_0_), custom_call_target="tpu_custom_call" | custom-call | flops 12884901888 | bytes 33554432 | tf_op jit(solution)/shard_map/right_terms/pallas_call | solution.py:142
  48.3 0.0 reduce-scatter.2.cloned.1.call-update
  48.3 0.0 all-gather.2.cloned.1.call-done
  48.3 1.9 %fusion = (bf16[2048,256]{1,0:T(8,128)(2,1)S(1)}, bf16[2048,256]{1,0:T(8,128)(2,1)S(1)}) fusion(f32[2048,256]{1,0:T(8,128)} %all-gather.2.cloned.1.call-done), kind=kLoop, calls=%fused_computation.2 | loop fusion | flops 2097152 | bytes 4194304 | tf_op jit(solution)/shard_map/convert_element_type | solution.py:194
  50.3 17.2 %left_terms.3 = f32[512,256]{1,0:T(8,128)S(1)} custom-call(s32[1]{0:T(128)} %bitcast.place_ref, f32[8,2048,1024]{2,1,0:T(8,128)} %matrices_ref.7, bf16[2048,256]{1,0:T(8,128)(2,1)S(1)} %get-tuple-element.12.high_ref, bf16[2048,256]{1,0:T(8,128)(2,1)S(1)} %get-tuple-element.11.low_ref, f32[8,256]{1,0:T(8,128)S(1)} %stack.40.weights_ref), custom_call_target="tpu_custom_call" | custom-call | flops 12884901888 | bytes 33554432 | tf_op jit(solution)/shard_map/left_terms/pallas_call | solution.py:163
  67.5 0.1 collective-permute-start.2
  67.6 17.3 %left_terms.2 = f32[512,256]{1,0:T(8,128)S(1)} custom-call(s32[1]{0:T(128)} %bitcast.8.place_ref, f32[8,2048,1024]{2,1,0:T(8,128)} %matrices_ref.7, bf16[2048,256]{1,0:T(8,128)(2,1)S(1)} %get-tuple-element.12.high_ref, bf16[2048,256]{1,0:T(8,128)(2,1)S(1)} %get-tuple-element.11.low_ref, f32[8,256]{1,0:T(8,128)S(1)} %stack.40.weights_ref), custom_call_target="tpu_custom_call" | custom-call | flops 12884901888 | bytes 33554432 | tf_op jit(solution)/shard_map/left_terms/pallas_call | solution.py:163
  84.9 0.0 collective-permute-done.2
  84.9 0.3 collective-permute-start.3
  85.2 0.0 reduce-scatter.2.cloned.1.call-done
  85.2 1.0 multiply_reduce_fusion.1
  86.2 0.3 collective-permute-done.3
  86.5 0.8 multiply_reduce_fusion
  87.3 13.4 %all_to_all.5 = f32[32,2,256]{2,1,0:T(2,128)S(1)} all-to-all(f32[32,2,256]{2,1,0:T(2,128)S(1)} %broadcast_in_dim.2), channel_id=1, replica_groups=mesh['row'=4,'col'=8] {'row','col'}, dimensions={0} | all-to-all | bytes 131072 | tf_op jit(solution)/shard_map/all_to_all | solution.py:230
  100.8 0.6 add_sqrt_fusion
  (5 shorter events, 0.1 us)
Async XLA Ops:
  7.2 41.2 %all-gather.2.cloned.1.call-start = ((), (), s32[]{:S(2)}) async-start(), calls=%async_computation.3 | async-start | bytes 2359296 | tf_op jit(solution)/shard_map/all_gather | solution.py:191
  7.9 77.3 %reduce-scatter.2.cloned.1.call-start = ((), (), s32[]{:S(2)}) async-start(), calls=%async_computation.2 | async-start | bytes 2359296 | tf_op jit(solution)/shard_map/reduce_scatter | solution.py:209
  7.9 2.6 %collective-permute-start = (f32[256,256]{1,0:T(8,128)}, f32[256,256]{1,0:T(8,128)S(1)}, u32[]{:S(2)}, u32[]{:S(2)}) collective-permute-start(f32[256,256]{1,0:T(8,128)} %param.6), channel_id=1, source_target_pairs={{0,8},{8,0},{16,24},{24,16},{1,9},{9,1},{17,25},{25,17},{2,10},{10... | collective-permute-start | bytes 786440 | tf_op jit(solution)/shard_map/ppermute | solution.py:179
  11.6 19.0 %collective-permute-start.1 = (f32[512,256]{1,0:T(8,128)S(1)}, f32[512,256]{1,0:T(8,128)S(1)}, u32[]{:S(2)}, u32[]{:S(2)}) collective-permute-start(f32[512,256]{1,0:T(8,128)S(1)} %maximum_select_fusion.vecs_ref), channel_id=1, source_target_pairs={{0,16},{8,24},{16,0},{24,8},{1,17},{9,25},{17,1},{25,9},{2,18},{10... | collective-permute-start | bytes 1572872 | tf_op jit(solution)/shard_map/ppermute | solution.py:179
  67.5 17.4 %collective-permute-start.2 = (f32[512,256]{1,0:T(8,128)S(1)}, f32[512,256]{1,0:T(8,128)S(1)}, u32[]{:S(2)}, u32[]{:S(2)}) collective-permute-start(f32[512,256]{1,0:T(8,128)S(1)} %left_terms.3), channel_id=1, source_target_pairs={{0,16},{8,24},{16,0},{24,8},{1,17},{9,25},{17,1},{25,9},{2,18},{10... | collective-permute-start | bytes 1572872 | tf_op jit(solution)/shard_map/ppermute | solution.py:179
  84.9 1.6 %collective-permute-start.3 = (f32[256,256]{1,0:T(8,128)S(1)}, f32[256,256]{1,0:T(8,128)S(1)}, u32[]{:S(2)}, u32[]{:S(2)}) collective-permute-start(f32[256,256]{1,0:T(8,128)S(1)} %dynamic-slice_add_fusion), channel_id=1, source_target_pairs={{0,8},{8,0},{16,24},{24,16},{1,9},{9,1},{17,25},{25,17},{2,10},{10... | collective-permute-start | bytes 786440 | tf_op jit(solution)/shard_map/ppermute | solution.py:179
Sparse Core Ops, SparseCore 0:
  9.5 36.0 all-gather.1
  48.5 33.2 reduce-scatter.1

commit v6 on v5

--- a/solution.py
+++ b/solution.py
@@ -48,6 +48,18 @@
     return copy
 
 
+def piece_copies(matrices_ref, place, buffer, sem):
+    width = buffer.shape[2]
+    columns = pl.ds(pl.multiple_of(place * width, width), width)
+    depth = matrices_ref.shape[1] // sem.shape[0]
+
+    def copy_piece(piece):
+        part = pl.ds(pl.multiple_of(piece * depth, depth), depth)
+        return pltpu.make_async_copy(matrices_ref.at[0, part, columns], buffer.at[0, part], sem.at[piece])
+
+    return copy_piece, depth
+
+
 def each_matrix(first, count, copy, step):
     def visit(term, carry):
         copy(term).wait()
@@ -68,14 +80,7 @@
     count, rows, _ = matrices_ref.shape
     chunk = rows // len(order)
     copy = block_copies(matrices_ref, place_ref[0], buffer, sem)
-    depth = 2 * chunk
-    width = buffer.shape[2]
-    columns = pl.ds(pl.multiple_of(place_ref[0] * width, width), width)
-
-    def copy_piece(piece):
-        part = pl.ds(pl.multiple_of(piece * depth, depth), depth)
-        return pltpu.make_async_copy(matrices_ref.at[0, part, columns], buffer.at[0, part], piece_sem.at[piece])
-
+    copy_piece, depth = piece_copies(matrices_ref, place_ref[0], buffer, piece_sem)
     for piece in range(rows // depth):
         copy_piece(jnp.int32(piece)).start()
     for term in range(1, min(SLOTS, count)):
@@ -106,14 +111,27 @@
     each_matrix(1, count, copy, step)
 
 
-def left_kernel(order, place_ref, matrices_ref, high_ref, low_ref, weights_ref, out_ref, buffer, sem):
+def left_kernel(order, place_ref, matrices_ref, high_ref, low_ref, weights_ref, out_ref, buffer, sem, piece_sem):
     count, rows, _ = matrices_ref.shape
     chunk = rows // len(order)
     copy = block_copies(matrices_ref, place_ref[0], buffer, sem)
-    for term in range(min(SLOTS, count)):
+    copy_piece, depth = piece_copies(matrices_ref, place_ref[0], buffer, piece_sem)
+    for piece in range(rows // depth):
+        copy_piece(jnp.int32(piece)).start()
+    for term in range(1, min(SLOTS, count)):
         copy(jnp.int32(term)).start()
     out_ref[...] = jnp.zeros_like(out_ref)
     at = [order.index(member) for member in range(len(order))]
+
+    def step_piece(piece, carry):
+        copy_piece(piece).wait()
+        block = buffer[0, pl.ds(pl.multiple_of(piece * depth, depth), depth), :]
+        places = [pl.ds(pl.multiple_of(i * chunk, chunk), chunk) for i in (piece, len(order) - 1 - piece)]
+        vecs = [jnp.concatenate([ref[place, :] for place in places], axis=0) for ref in (high_ref, low_ref)]
+        out_ref[...] += product(halves(block), vecs, ((0,), (0,))) * weights_ref[0:1, :]
+        return carry
+
+    lax.fori_loop(0, rows // depth, step_piece, 0)
 
     def step(term):
         vecs = [
@@ -122,7 +140,7 @@
         terms = product(halves(buffer[lax.rem(term, SLOTS)]), vecs, ((0,), (0,)))
         out_ref[...] += terms * weights_ref[pl.ds(term, 1), :]
 
-    each_matrix(0, count, copy, step)
+    each_matrix(1, count, copy, step)
 
 
 VMEM = pl.BlockSpec(memory_space=pltpu.VMEM)
@@ -168,6 +186,7 @@
         scratch_shapes=[
             pltpu.VMEM((SLOTS, rows, width), jnp.float32),
             pltpu.SemaphoreType.DMA((SLOTS,)),
+            pltpu.SemaphoreType.DMA((len(order) // 2,)),
         ],
         compiler_params=pltpu.CompilerParams(vmem_limit_bytes=VMEM_LIMIT),
         cost_estimate=cost(count, rows, width, trip),

time: 108 us -> 108 us (level)
  no operation moved by 1% of the time
where the time goes in v6:
time: 108 us
  Pallas kernels  68 us (63%)
  between operations  14.1 us (13%)
  blocking collectives  13.4 us (12%)
  other arithmetic  6.82 us (6%)
  starting transfers between devices  3.58 us (3%)
    pallas_call x2, Pallas kernels, right_terms(): pl.pallas_call(functools.partial(right_kernel, order, total is not None),...  34 us
    pallas_call x2, Pallas kernels, left_terms(): pl.pallas_call(functools.partial(left_kernel, order), out_shape=jax.Shape...  33.9 us
    all_to_all x1, blocking collectives, body(): lax.all_to_all(copies, ('row', 'col'), split_axis=0, concat_axis=0, tiled...  13.4 us
    ppermute x4, starting transfers between devices, exchange(): return lax.ppermute(values, axis, [(i, i ^ bit) for i in range(size)])  3.5 us
  transfers between devices with their start and end apart: 6, of which 1 were waited for; matrix products, arithmetic and copies ran while one was open for 6% of the time, Pallas kernels for 63%

profile of v6, /device:TPU:0, one launch (start us, length us, event | category | flops | bytes accessed | tf_op | source)
XLA Modules:
  0.0 107.7 jit_solution(11321187121438933440)
XLA Ops:
  7.2 0.0 all-gather.2.cloned.1.call-start
  7.2 0.7 all-gather.2.cloned.1.call-update
  7.9 0.0 reduce-scatter.2.cloned.1.call-start
  7.9 0.5 collective-permute-start
  8.5 0.7 multiply_subtract_fusion
  9.2 0.7 multiply_subtract_fusion.1
  9.8 0.7 stack.40.weights_ref
  10.6 0.0 collective-permute-done
  10.6 1.1 %maximum_select_fusion.vecs_ref = f32[512,256]{1,0:T(8,128)S(1)} fusion(f32[256,256]{1,0:T(8,128)S(1)} %collective-permute-done, f32[256,256]{1,0:T(8,128)} %param.6, pred[]{:T(512)S(6)} %eq.3), kind=kLoop, calls=%fused_computation.3 | loop fusion | flops 393216 | bytes 1048577 | tf_op jit(solution)/shard_map/jit(_where)/select_n | solution.py:221
  11.6 2.6 %collective-permute-start.1 = (f32[512,256]{1,0:T(8,128)S(1)}, f32[512,256]{1,0:T(8,128)S(1)}, u32[]{:S(2)}, u32[]{:S(2)}) collective-permute-start(f32[512,256]{1,0:T(8,128)S(1)} %maximum_select_fusion.vecs_ref), channel_id=1, source_target_pairs={{0,16},{8,24},{16,0},{24,8},{1,17},{9,25},{17,1},{25,9},{2,18},{10... | collective-permute-start | bytes 1572872 | tf_op jit(solution)/shard_map/ppermute | solution.py:198
  14.2 16.4 %right_terms.2.rest_0_ = f32[2048,256]{1,0:T(8,128)S(1)} custom-call(s32[1]{0:T(128)} %bitcast.8.place_ref, f32[8,2048,1024]{2,1,0:T(8,128)} %matrices_ref.7, f32[512,256]{1,0:T(8,128)S(1)} %maximum_select_fusion.vecs_ref, f32[8,256]{1,0:T(8,128)S(1)} %stack.40.weights_ref), custom_call_target="tpu_custom_call" | custom-call | flops 12884901888 | bytes 33554432 | tf_op jit(solution)/shard_map/right_terms/pallas_call | solution.py:160
  30.7 0.0 collective-permute-done.1.vecs_ref
  30.7 17.6 %right_terms.3 = f32[2048,256]{1,0:T(8,128)} custom-call(s32[1]{0:T(128)} %bitcast.place_ref, f32[8,2048,1024]{2,1,0:T(8,128)} %matrices_ref.7, f32[512,256]{1,0:T(8,128)S(1)} %collective-permute-done.1.vecs_ref, f32[8,256]{1,0:T(8,128)S(1)} %stack.40.weights_ref, f32[2048,256]{1,0:T(8,128)S(1)} %right_terms.2.rest_0_), custom_call_target="tpu_custom_call" | custom-call | flops 12884901888 | bytes 33554432 | tf_op jit(solution)/shard_map/right_terms/pallas_call | solution.py:160
  48.3 0.0 reduce-scatter.2.cloned.1.call-update
  48.3 0.0 all-gather.2.cloned.1.call-done
  48.3 1.9 %fusion = (bf16[2048,256]{1,0:T(8,128)(2,1)S(1)}, bf16[2048,256]{1,0:T(8,128)(2,1)S(1)}) fusion(f32[2048,256]{1,0:T(8,128)} %all-gather.2.cloned.1.call-done), kind=kLoop, calls=%fused_computation.2 | loop fusion | flops 2097152 | bytes 4194304 | tf_op jit(solution)/shard_map/convert_element_type | solution.py:213
  50.3 17.0 %left_terms.3 = f32[512,256]{1,0:T(8,128)S(1)} custom-call(s32[1]{0:T(128)} %bitcast.place_ref, f32[8,2048,1024]{2,1,0:T(8,128)} %matrices_ref.7, bf16[2048,256]{1,0:T(8,128)(2,1)S(1)} %get-tuple-element.12.high_ref, bf16[2048,256]{1,0:T(8,128)(2,1)S(1)} %get-tuple-element.11.low_ref, f32[8,256]{1,0:T(8,128)S(1)} %stack.40.weights_ref), custom_call_target="tpu_custom_call" | custom-call | flops 12884901888 | bytes 33554432 | tf_op jit(solution)/shard_map/left_terms/pallas_call | solution.py:181
  67.2 0.1 collective-permute-start.2
  67.3 17.0 %left_terms.2 = f32[512,256]{1,0:T(8,128)S(1)} custom-call(s32[1]{0:T(128)} %bitcast.8.place_ref, f32[8,2048,1024]{2,1,0:T(8,128)} %matrices_ref.7, bf16[2048,256]{1,0:T(8,128)(2,1)S(1)} %get-tuple-element.12.high_ref, bf16[2048,256]{1,0:T(8,128)(2,1)S(1)} %get-tuple-element.11.low_ref, f32[8,256]{1,0:T(8,128)S(1)} %stack.40.weights_ref), custom_call_target="tpu_custom_call" | custom-call | flops 12884901888 | bytes 33554432 | tf_op jit(solution)/shard_map/left_terms/pallas_call | solution.py:181
  84.3 0.0 collective-permute-done.2
  84.4 0.3 collective-permute-start.3
  84.7 0.0 reduce-scatter.2.cloned.1.call-done
  84.7 1.0 multiply_reduce_fusion.1
  85.7 0.3 collective-permute-done.3
  86.0 0.8 multiply_reduce_fusion
  86.8 13.4 %all_to_all.5 = f32[32,2,256]{2,1,0:T(2,128)S(1)} all-to-all(f32[32,2,256]{2,1,0:T(2,128)S(1)} %broadcast_in_dim.2), channel_id=1, replica_groups=mesh['row'=4,'col'=8] {'row','col'}, dimensions={0} | all-to-all | bytes 131072 | tf_op jit(solution)/shard_map/all_to_all | solution.py:249
  100.2 0.6 add_sqrt_fusion
  (5 shorter events, 0.1 us)
Async XLA Ops:
  7.2 41.2 %all-gather.2.cloned.1.call-start = ((), (), s32[]{:S(2)}) async-start(), calls=%async_computation.3 | async-start | bytes 2359296 | tf_op jit(solution)/shard_map/all_gather | solution.py:210
  7.9 76.8 %reduce-scatter.2.cloned.1.call-start = ((), (), s32[]{:S(2)}) async-start(), calls=%async_computation.2 | async-start | bytes 2359296 | tf_op jit(solution)/shard_map/reduce_scatter | solution.py:228
  7.9 2.6 %collective-permute-start = (f32[256,256]{1,0:T(8,128)}, f32[256,256]{1,0:T(8,128)S(1)}, u32[]{:S(2)}, u32[]{:S(2)}) collective-permute-start(f32[256,256]{1,0:T(8,128)} %param.6), channel_id=1, source_target_pairs={{0,8},{8,0},{16,24},{24,16},{1,9},{9,1},{17,25},{25,17},{2,10},{10... | collective-permute-start | bytes 786440 | tf_op jit(solution)/shard_map/ppermute | solution.py:198
  11.6 19.0 %collective-permute-start.1 = (f32[512,256]{1,0:T(8,128)S(1)}, f32[512,256]{1,0:T(8,128)S(1)}, u32[]{:S(2)}, u32[]{:S(2)}) collective-permute-start(f32[512,256]{1,0:T(8,128)S(1)} %maximum_select_fusion.vecs_ref), channel_id=1, source_target_pairs={{0,16},{8,24},{16,0},{24,8},{1,17},{9,25},{17,1},{25,9},{2,18},{10... | collective-permute-start | bytes 1572872 | tf_op jit(solution)/shard_map/ppermute | solution.py:198
  67.2 17.1 %collective-permute-start.2 = (f32[512,256]{1,0:T(8,128)S(1)}, f32[512,256]{1,0:T(8,128)S(1)}, u32[]{:S(2)}, u32[]{:S(2)}) collective-permute-start(f32[512,256]{1,0:T(8,128)S(1)} %left_terms.3), channel_id=1, source_target_pairs={{0,16},{8,24},{16,0},{24,8},{1,17},{9,25},{17,1},{25,9},{2,18},{10... | collective-permute-start | bytes 1572872 | tf_op jit(solution)/shard_map/ppermute | solution.py:198
  84.4 1.6 %collective-permute-start.3 = (f32[256,256]{1,0:T(8,128)S(1)}, f32[256,256]{1,0:T(8,128)S(1)}, u32[]{:S(2)}, u32[]{:S(2)}) collective-permute-start(f32[256,256]{1,0:T(8,128)S(1)} %dynamic-slice_add_fusion), channel_id=1, source_target_pairs={{0,8},{8,0},{16,24},{24,16},{1,9},{9,1},{17,25},{25,17},{2,10},{10... | collective-permute-start | bytes 786440 | tf_op jit(solution)/shard_map/ppermute | solution.py:198
Sparse Core Ops, SparseCore 0:
  9.5 36.0 all-gather.1
  48.5 33.2 reduce-scatter.1
